TPU v7x, 128 devices: a whole 4x4x4 slice. The times are simulated.
128 devices in a mesh: row: 16 (over z_lo, x, core), col: 8 (over y, z_hi).
Axes of the slice: x: 4, y: 4, z: 4 (z_hi: 2, z_lo: 2; z = z_hi * 2 + z_lo), core: 2. Of those that a mesh axis runs over, the one named last changes fastest.
Arguments:
- tile_u: float32 [16, 32, 2048, 128], P('row', 'col'), may hold values from -6 to 6
- tile_v: float32 [16, 32, 2048, 128], P('row', 'col'), may hold values from -1.5 to 1.5
- row_panel_u: float32 [16, 2048, 128], P('row', 'col'), may hold values from -6 to 6
- row_panel_v: float32 [16, 2048, 128], P('row', 'col'), may hold values from -0.125 to 0.125
- col_panel_u: float32 [32, 2048, 128], P('row', 'col'), may hold values from -6 to 6
- col_panel_v: float32 [32, 2048, 128], P('row', 'col'), may hold values from -0.125 to 0.125
- diag_inverse: float32 [2048, 2048], P('col'), may hold values from -0.15 to 2, as said below
- sketch: float32 [2048, 128], replicated, may hold values from -0.125 to 0.125
Outputs:
- new_u: float32 [16, 32, 2048, 128], P('row', 'col')
- new_v: float32 [16, 32, 2048, 128], P('row', 'col')
Inputs may be any that keep to these rules, and one draw needn't show every extreme that they name: `diag_inverse`: lower triangular; the diagonal lies between 0.5 and 2, the entries below it between -0.15 and 0.15.
All inputs are finite; a program needn't handle non-finite values.
Results may differ from a plain program's by a relative error of at most 0.0003.
Values sent between devices are 32-bit elements; how exact they have to be, the bound alone decides.
A program may use at most 128 MiB of HBM per device.

v0:
```python
import math

import jax
import jax.numpy as jnp
from jax import lax
from jax.experimental import pallas as pl
from jax.experimental.pallas import tpu as pltpu
from jax.sharding import PartitionSpec as P

highest = lax.Precision.HIGHEST
f32, bf16 = jnp.float32, jnp.bfloat16


def halves(x):
    hi = x.astype(bf16)
    lo = (x - hi.astype(f32)).astype(bf16)
    return jnp.concatenate([hi, lo], axis=1)


def fold4(q):
    k = q.shape[0] // 2
    n = q.shape[1] // 2
    return q[:k, :n] + q[:k, n:] + q[k:, :n] + q[k:, n:]


def doubled(w):
    h = halves(w)
    return jnp.concatenate([h, h], axis=0)


def dot(a, b, ca=1, cb=0, precision=highest):
    return lax.dot_general(a, b, (((ca,), (cb,)), ((), ())), precision=precision, preferred_element_type=f32)


def dotb(a, b, ca=1, cb=0):
    return lax.dot_general(a, b, (((ca,), (cb,)), ((), ())), preferred_element_type=f32)


def inverse_factors(gram_ref, inv_ref, fac_ref):
    tiles, k, _ = gram_ref.shape
    row = lax.broadcasted_iota(jnp.int32, (tiles, 8, k), 1)
    lane = lax.broadcasted_iota(jnp.int32, (tiles, 8, k), 2)
    for p in range(k // 8):
        lo = 8 * p
        panel = gram_ref[:, lo : lo + 8, :]
        if p == 0:
            own = jnp.zeros((tiles, 8, k), f32)
        else:
            own = inv_ref[:, lo : lo + 8, :]
        own = own + jnp.where(lane == row + lo, 1.0, 0.0)
        cols = [jnp.broadcast_to(panel[:, :, lo + i : lo + i + 1], panel.shape) for i in range(8)]
        scale = jnp.zeros((tiles, 8, k), f32)
        pivot = jnp.zeros((tiles, 8, k), f32)
        for i in range(8):
            piv = jnp.broadcast_to(cols[i][:, i : i + 1, :], panel.shape)
            recip = 1.0 / piv
            scale = jnp.where(row == i, recip, scale)
            if i < 7:
                m = jnp.where(row > i, cols[i] * recip, 0.0)
                for j in range(i + 1, 8):
                    cols[j] = cols[j] - m * cols[j][:, i : i + 1, :]
                panel = panel - m * panel[:, i : i + 1, :]
                own = own - m * own[:, i : i + 1, :]
        fac_ref[:, lo : lo + 8, :] = own * jnp.sqrt(scale)
        if p < k // 8 - 1:
            lower = panel * scale
            for t in range(tiles):
                both = jnp.concatenate([panel[t], own[t]], axis=1)
                upd = dot(lower[t], both, 0, 0)
                gram_ref[t, lo + 8 :, :] = gram_ref[t, lo + 8 :, :] - upd[lo + 8 :, :k]
                if p == 0:
                    inv_ref[t, lo + 8 :, :] = -upd[lo + 8 :, k:]
                else:
                    inv_ref[t, lo + 8 :, :] = inv_ref[t, lo + 8 :, :] - upd[lo + 8 :, k:]


def local_kernel(u_hbm, v_hbm, r_ref, c_hbm, cores_ref, s_ref, nu_hbm, nv_hbm,
                 ubuf, vbuf, cbuf, usp, vsp, csp, rsp, tt, w_s, t_s, gram_s, inv_s, fac_s, in_sem, out_sem):
    tiles, rows, k = ubuf.shape
    step = min(512, rows)
    scaling = math.sqrt(rows)

    def load(t, which):
        src, dst = ((u_hbm, ubuf), (v_hbm, vbuf), (c_hbm, cbuf))[which]
        return pltpu.make_async_copy(src.at[t], dst.at[t], in_sem.at[which, t])

    for t in range(tiles):
        for which in range(3):
            load(t, which).start()

    for lo in range(0, rows, step):
        for n, ref in enumerate((r_ref, s_ref)):
            h = halves(ref[lo : lo + step, :])
            if n == 0:
                rsp[lo : lo + step, :] = h
            tt[n, :, lo : lo + step] = h.astype(f32).T.astype(bf16)
    rr = fold4(dotb(tt[0], rsp[...]))

    for t in range(tiles):
        for which in range(3):
            load(t, which).wait()
            buf, sp = ((ubuf, usp), (vbuf, vsp), (cbuf, csp))[which]

            def body(n, carry, buf=buf, sp=sp, t=t):
                at = pl.ds(pl.multiple_of(n * step, step), step)
                sp[t, at, :] = halves(buf[t, at, :])
                return carry

            lax.fori_loop(0, rows // step, body, 0)
        uu = fold4(dotb(usp[t], usp[t], 0, 0))
        ru = fold4(dotb(tt[0], usp[t]))
        p1t = fold4(dotb(tt[1], vsp[t]))
        p2t = fold4(dotb(tt[1], csp[t]))
        cores = cores_ref[t]
        w1 = p1t.T
        w2 = -dot(cores, p2t, 1, 1)
        w = jnp.concatenate([w1, w2], axis=0)
        g = jnp.concatenate([jnp.concatenate([uu, ru.T], axis=1), jnp.concatenate([ru, rr], axis=1)], axis=0)
        tw = dot(g, w)
        w_s[t] = w
        t_s[t] = tw
        gram_s[t] = dot(w, tw, 0, 0)

    inverse_factors(gram_s, inv_s, fac_s)

    def store(t, which):
        src, dst = ((ubuf, nu_hbm), (vbuf, nv_hbm))[which]
        return pltpu.make_async_copy(src.at[t], dst.at[t], out_sem.at[which, t])

    for t in range(tiles):
        fac = fac_s[t]
        x = dot(w_s[t], fac, 1, 1) * scaling
        y = dot(t_s[t], fac, 1, 1) * (1.0 / scaling)
        c1 = y[:k]
        c2 = -dot(cores_ref[t], y[k:], 0, 0)
        x1, x2, c1, c2 = doubled(x[:k]), doubled(x[k:]), doubled(c1), doubled(c2)

        def finish(n, carry, t=t, x1=x1, x2=x2, c1=c1, c2=c2):
            at = pl.ds(pl.multiple_of(n * step, step), step)
            a = dotb(usp[t, at, :], x1) + dotb(rsp[at, :], x2)
            ubuf[t, at, :] = a[:, :k] + a[:, k:]
            b = dotb(vsp[t, at, :], c1) + dotb(csp[t, at, :], c2)
            vbuf[t, at, :] = b[:, :k] + b[:, k:]
            return carry

        lax.fori_loop(0, rows // step, finish, 0)
        store(t, 0).start()
        store(t, 1).start()
    for t in range(tiles):
        store(t, 0).wait()
        store(t, 1).wait()


def recompress(tile_u, tile_v, row_u, col_u, cores, sketch):
    tiles, rows, k = tile_u.shape
    vm = pl.BlockSpec(memory_space=pltpu.VMEM)
    hbm = pl.BlockSpec(memory_space=pl.ANY)
    out = jax.ShapeDtypeStruct(tile_u.shape, f32)
    return pl.pallas_call(
        local_kernel,
        name="recompress",
        out_shape=(out, out),
        in_specs=[hbm, hbm, vm, hbm, vm, vm],
        out_specs=(hbm, hbm),
        scratch_shapes=[
            pltpu.VMEM((tiles, rows, k), f32),
            pltpu.VMEM((tiles, rows, k), f32),
            pltpu.VMEM((tiles, rows, k), f32),
            pltpu.VMEM((tiles, rows, 2 * k), bf16),
            pltpu.VMEM((tiles, rows, 2 * k), bf16),
            pltpu.VMEM((tiles, rows, 2 * k), bf16),
            pltpu.VMEM((rows, 2 * k), bf16),
            pltpu.VMEM((2, 2 * k, rows), bf16),
            pltpu.VMEM((tiles, 2 * k, k), f32),
            pltpu.VMEM((tiles, 2 * k, k), f32),
            pltpu.VMEM((tiles, k, k), f32),
            pltpu.VMEM((tiles, k, k), f32),
            pltpu.VMEM((tiles, k, k), f32),
            pltpu.SemaphoreType.DMA((3, tiles)),
            pltpu.SemaphoreType.DMA((2, tiles)),
        ],
        compiler_params=pltpu.CompilerParams(vmem_limit_bytes=50 * 2**20),
        cost_estimate=pl.CostEstimate(flops=10**10, bytes_accessed=24 * 2**20, transcendentals=0),
    )(tile_u, tile_v, row_u, col_u, cores, sketch)


def side_by_side(arrays, axis, dim, along):
    widths = [a.shape[along] for a in arrays]
    both = jnp.concatenate(arrays, axis=along)
    filled = lax.all_gather(both, axis, axis=dim, tiled=True)
    return tuple(jnp.split(filled, [sum(widths[:k]) for k in range(1, len(widths))], axis=along))


def laid_out(parts, dim):
    parts = jnp.moveaxis(parts, 0, dim)
    shape = parts.shape
    return parts.reshape(*shape[:dim], shape[dim] * shape[dim + 1], *shape[dim + 2 :])


def from_everyone(x, axis):
    copies = jnp.broadcast_to(x, (lax.axis_size(axis), *x.shape))
    return lax.all_to_all(copies, axis, split_axis=0, concat_axis=0, tiled=True)


def gather_directly(x, axis, dim):
    return laid_out(from_everyone(x, axis), dim)


def split_up(x, dim, count):
    shape = x.shape
    parts = x.reshape(*shape[:dim], count, shape[dim] // count, *shape[dim + 1 :])
    return jnp.moveaxis(parts, dim, 0)


def sum_at_owner(x, axis, dim):
    parts = split_up(x, dim, lax.axis_size(axis))
    arrived = lax.all_to_all(parts, axis, split_axis=0, concat_axis=0, tiled=True)
    return arrived.sum(axis=0)


def body(tile_u, tile_v, row_panel_u, row_panel_v, col_panel_u, col_panel_v, diag_inverse, sketch):
    pieces = side_by_side((row_panel_v, col_panel_v), "col", 1, 0)
    first = jnp.einsum("ab,tbk->tak", diag_inverse, pieces[0], precision=highest)
    second = jnp.einsum("ab,tbk->tak", diag_inverse, pieces[1], precision=highest)
    col_u_rows, col_v_rows = side_by_side((col_panel_u, second), "row", 0, 1)
    row_u_full = gather_directly(row_panel_u, "col", 1)
    col_u_full = lax.all_to_all(col_u_rows, "col", split_axis=0, concat_axis=1, tiled=True)
    partial_cores = jnp.einsum("iak,jal->ijkl", first, col_v_rows, precision=highest)
    cores = sum_at_owner(partial_cores, "col", 1)
    new_u, new_v = recompress(tile_u[0], tile_v[0], row_u_full[0], col_u_full, cores[0], sketch)
    return new_u[None], new_v[None]


def solution(mesh):
    in_specs = (
        P("row", "col", None, None),
        P("row", "col", None, None),
        P("row", "col", None),
        P("row", "col", None),
        P("row", "col", None),
        P("row", "col", None),
        P("col", None),
        P(),
    )
    out_specs = (P("row", "col", None, None), P("row", "col", None, None))
    return jax.shard_map(body, mesh=mesh, in_specs=in_specs, out_specs=out_specs, check_vma=False)
```

profile of v0, /device:TPU:1, one launch (start us, length us, event | category | flops | bytes accessed | tf_op | source)
XLA Modules:
  0.0 302.1 jit_solution(4376012294517844648)
XLA Ops:
  7.2 0.0 copy-start
  7.2 0.0 all-gather.3.cloned.1.call-start
  7.2 1.2 copy.16
  8.4 1.0 copy.15
  9.5 0.8 pad_maximum_fusion.1
  10.2 0.0 all-gather.3.cloned.1.call-update
  10.3 0.0 all-gather.5.cloned.1.call-start
  10.3 1.1 copy.17
  11.4 69.6 %all-gather.3.cloned.1.call-done = f32[3,2048,128]{1,2,0:T(8,128)} async-done(((f32[3,256,128]{1,2,0:T(8,128)}), f32[3,2048,128]{1,2,0:T(8,128)}) %all-gather.3.cloned.1.call-update) | async-done | bytes 3145744 | tf_op jit(solution)/shard_map/all_gather | solution.py:190
  81.0 0.0 copy-done
  81.0 3.5 %fusion.4 = f32[2,256,128]{1,2,0:T(8,128)S(1)} fusion(f32[3,2048,128]{1,2,0:T(8,128)} %all-gather.3.cloned.1.call-done, f32[256,2048]{1,0:T(8,128)S(1)} %copy-done), kind=kOutput, calls=%fused_computation.5 | convolution fusion | flops 1610612736 | bytes 5505024 | tf_op jit(solution)/shard_map/ab,tbk->tak/dot_general | solution.py:224
  84.4 0.1 pad_maximum_fusion
  84.5 1.0 copy.18
  85.5 0.0 all-gather.5.cloned.1.call-update
  85.5 3.4 %convolution_bitcast_fusion = f32[256,128,1]{0,1,2:T(8,128)S(1)} fusion(f32[256,2048]{1,0:T(8,128)S(1)} %copy-done, f32[3,2048,128]{1,2,0:T(8,128)} %all-gather.3.cloned.1.call-done), kind=kOutput, calls=%fused_computation.6 | convolution fusion | flops 805306368 | bytes 3276800 | tf_op jit(solution)/shard_map/ab,tbk->tak/dot_general | solution.py:223
  89.0 48.8 %all-gather.5.cloned.1.call-done = f32[32,512,128]{2,1,0:T(8,128)} async-done(((f32[2,512,128]{2,1,0:T(8,128)}), f32[32,512,128]{2,1,0:T(8,128)}) %all-gather.5.cloned.1.call-update) | async-done | bytes 8388624 | tf_op jit(solution)/shard_map/all_gather | solution.py:190
  137.8 10.2 %fusion = f32[32,128,128]{2,1,0:T(8,128)} fusion(f32[256,128,1]{0,1,2:T(8,128)S(1)} %convolution_bitcast_fusion, f32[32,512,128]{2,1,0:T(8,128)} %all-gather.5.cloned.1.call-done), kind=kOutput, calls=%fused_computation | convolution fusion | flops 1610612736 | bytes 6422528 | tf_op jit(solution)/shard_map/iak,jal->ijkl/dot_general | solution.py:228
  148.0 6.4 %all-to-all-start.2 = ((f32[8,1,4,128,128]{3,4,2,1,0:T(8,128)}), f32[8,1,4,128,128]{3,4,2,1,0:T(8,128)}, u32[]{:S(2)}, u32[]{:S(2)}) async-start(f32[8,1,4,128,128]{3,4,2,1,0:T(8,128)} %bitcast.42), calls=%async_computation.2 | async-start | bytes 4194304 | tf_op jit(solution)/shard_map/all_to_all | solution.py:217
  154.4 4.7 %split.16 = f32[32,256,128]{2,1,0:T(8,128)} slice(f32[32,512,128]{2,1,0:T(8,128)} %all-gather.5.cloned.1.call-done), slice={[0:32], [0:256], [0:128]} | slice | bytes 8388608 | tf_op jit(solution)/shard_map/split | solution.py:191
  159.0 0.0 copy-start.2
  159.0 26.4 %all-to-all-done.2 = f32[8,1,4,128,128]{3,4,2,1,0:T(8,128)} async-done(((f32[8,1,4,128,128]{3,4,2,1,0:T(8,128)}), f32[8,1,4,128,128]{3,4,2,1,0:T(8,128)}, u32[]{:S(2)}, u32[]{:S(2)}) %all-to-all-start.2) | async-done | bytes 2097184 | tf_op jit(solution)/shard_map/all_to_all | solution.py:217
  185.5 53.2 %all_to_all.28 = f32[32,256,128]{2,1,0:T(8,128)} all-to-all(f32[32,256,128]{2,1,0:T(8,128)} %split.16), channel_id=1, replica_groups=mesh['row'=16,'col'=8] {'col'}, dimensions={0} | all-to-all | bytes 8388608 | tf_op jit(solution)/shard_map/all_to_all | solution.py:227
  238.7 0.0 copy-done.2
  238.7 1.0 broadcast_in_dim.9
  239.7 3.7 %all-to-all-start = ((f32[8,1,256,128]{3,2,1,0:T(8,128)}), f32[8,1,256,128]{3,2,1,0:T(8,128)S(1)}, u32[]{:S(2)}, u32[]{:S(2)}) async-start(f32[8,1,256,128]{3,2,1,0:T(8,128)} %broadcast_in_dim.9), calls=%async_computation | async-start | bytes 2097152 | tf_op jit(solution)/shard_map/all_to_all | solution.py:202
  243.5 2.4 bitcast_reduce_fusion
  245.9 1.1 copy.24.cores_ref
  247.0 4.6 %copy.19 = f32[8,4,256,128]{3,2,0,1:T(8,128)} copy(f32[8,4,256,128]{3,2,1,0:T(8,128)} %bitcast.41) | data formatting | bytes 8388608 | tf_op jit(solution)/shard_map/all_to_all | solution.py:227
  251.6 5.7 %all-to-all-done = f32[8,1,256,128]{3,2,1,0:T(8,128)S(1)} async-done(((f32[8,1,256,128]{3,2,1,0:T(8,128)}), f32[8,1,256,128]{3,2,1,0:T(8,128)S(1)}, u32[]{:S(2)}, u32[]{:S(2)}) %all-to-all-start) | async-done | bytes 1048608 | tf_op jit(solution)/shard_map/all_to_all | solution.py:202
  257.3 0.0 copy-start.1
  257.3 1.2 copy-done.1
  258.5 36.7 %recompress.1 = (f32[4,2048,128]{2,1,0:T(8,128)}, f32[4,2048,128]{2,1,0:T(8,128)}) custom-call(f32[4,2048,128]{2,1,0:T(8,128)} %bitcast.45, f32[4,2048,128]{2,1,0:T(8,128)} %bitcast.46, f32[2048,128]{1,0:T(8,128)S(1)} %bitcast.40, f32[4,2048,128]{2,1,0:T(8,128)} %bitcast.43, f32[4,128,128]{2,1,0:T(8,128)S(1)} %copy.24.cores_ref, f32[2048,128]{1,0:T(8,128)S(1)} %copy-done.1), custom_call_target="tpu_custom_call" | custom-call | flops 10000000000 | bytes 25165824 | tf_op jit(solution)/shard_map/recompress/pallas_call | solution.py:159
Async XLA Ops:
  7.2 73.8 %copy-start = (f32[256,2048]{1,0:T(8,128)S(1)}, f32[256,2048]{1,0:T(8,128)}, u32[]{:S(2)}) copy-start(f32[256,2048]{1,0:T(8,128)} %param.14) | copy-start | bytes 6291460
  7.2 73.8 %all-gather.3.cloned.1.call-start = ((), (), s32[]{:S(2)}) async-start(), calls=%async_computation.3 | async-start | bytes 3538944 | tf_op jit(solution)/shard_map/all_gather | solution.py:190
  10.3 127.5 %all-gather.5.cloned.1.call-start = ((), (), s32[]{:S(2)}) async-start(), calls=%async_computation.4 | async-start | bytes 8912896 | tf_op jit(solution)/shard_map/all_gather | solution.py:190
  148.0 37.5 %all-to-all-start.2 = ((f32[8,1,4,128,128]{3,4,2,1,0:T(8,128)}), f32[8,1,4,128,128]{3,4,2,1,0:T(8,128)}, u32[]{:S(2)}, u32[]{:S(2)}) async-start(f32[8,1,4,128,128]{3,4,2,1,0:T(8,128)} %bitcast.42), calls=%async_computation.2 | async-start | bytes 4194304 | tf_op jit(solution)/shard_map/all_to_all | solution.py:217
  159.0 79.6 %copy-start.2 = (f32[1,256,128]{2,1,0:T(8,128)S(1)}, f32[1,256,128]{2,1,0:T(8,128)}, u32[]{:S(2)}) copy-start(f32[1,256,128]{2,1,0:T(8,128)} %param.10) | copy-start | bytes 393220
  239.7 17.6 %all-to-all-start = ((f32[8,1,256,128]{3,2,1,0:T(8,128)}), f32[8,1,256,128]{3,2,1,0:T(8,128)S(1)}, u32[]{:S(2)}, u32[]{:S(2)}) async-start(f32[8,1,256,128]{3,2,1,0:T(8,128)} %broadcast_in_dim.9), calls=%async_computation | async-start | bytes 2097152 | tf_op jit(solution)/shard_map/all_to_all | solution.py:202
  257.3 1.2 copy-start.1
Sparse Core Ops, SparseCore 0:
  10.8 70.1 all-gather.2
  85.6 52.0 all-gather.4
where the time goes:
time: 305 us; the launch traced here: 302 us
  waiting for transfers between devices  151 us (50%)
  blocking collectives  53.2 us (17%)
  Pallas kernels  36.7 us (12%)
  matrix products  17.1 us (6%)
  local copies, waits for them, and re-layouts  16.9 us (6%)
  between operations  14.1 us (5%)
  starting transfers between devices  10.2 us (3%)
  other arithmetic  3.25 us (1%)
    all_gather x2, waiting for transfers between devices, side_by_side(): filled = lax.all_gather(both, axis, axis=dim, tiled=True)  118 us
    all_to_all x1, blocking collectives, body(): lax.all_to_all(col_u_rows, 'col', split_axis=0, concat_axis=1, tiled=True)  53.2 us
    pallas_call x1, Pallas kernels, recompress(): pl.pallas_call(local_kernel, name='recompress', out_shape=(out, out), in_...  36.7 us
    all_to_all x1, waiting for transfers between devices, sum_at_owner(): lax.all_to_all(parts, axis, split_axis=0, concat_axis=0, tiled=True)  26.4 us
    dot_general x1, matrix products, body(): jnp.einsum('iak,jal->ijkl', first, col_v_rows, precision=highest)  10.2 us
    all_to_all x1, starting transfers between devices, sum_at_owner(): lax.all_to_all(parts, axis, split_axis=0, concat_axis=0, tiled=True)  6.42 us
  transfers between devices with their start and end apart: 4, of which 4 were waited for; matrix products, arithmetic and copies ran while one was open for 6% of the time, Pallas kernels for 0%

commit v1 on v0

--- a/solution.py
+++ b/solution.py
@@ -184,50 +184,363 @@
     )(tile_u, tile_v, row_u, col_u, cores, sketch)
 
 
-def side_by_side(arrays, axis, dim, along):
-    widths = [a.shape[along] for a in arrays]
-    both = jnp.concatenate(arrays, axis=along)
-    filled = lax.all_gather(both, axis, axis=dim, tiled=True)
-    return tuple(jnp.split(filled, [sum(widths[:k]) for k in range(1, len(widths))], axis=along))
-
-
-def laid_out(parts, dim):
-    parts = jnp.moveaxis(parts, 0, dim)
-    shape = parts.shape
-    return parts.reshape(*shape[:dim], shape[dim] * shape[dim + 1], *shape[dim + 2 :])
-
-
-def from_everyone(x, axis):
-    copies = jnp.broadcast_to(x, (lax.axis_size(axis), *x.shape))
-    return lax.all_to_all(copies, axis, split_axis=0, concat_axis=0, tiled=True)
-
-
-def gather_directly(x, axis, dim):
-    return laid_out(from_everyone(x, axis), dim)
-
-
-def split_up(x, dim, count):
-    shape = x.shape
-    parts = x.reshape(*shape[:dim], count, shape[dim] // count, *shape[dim + 1 :])
-    return jnp.moveaxis(parts, dim, 0)
-
-
-def sum_at_owner(x, axis, dim):
-    parts = split_up(x, dim, lax.axis_size(axis))
-    arrived = lax.all_to_all(parts, axis, split_axis=0, concat_axis=0, tiled=True)
-    return arrived.sum(axis=0)
+MESH = pl.DeviceIdType.MESH
+CENTRE, ACROSS, LEFT, RIGHT = 0, 1, 0, 1
+
+
+class Links:
+    def __init__(self, cols):
+        self.r = lax.axis_index("row")
+        self.c = lax.axis_index("col")
+        self.cols = cols
+        self.core = lax.rem(self.r, 2)
+        self.m = lax.div(self.r, 2)
+        self.x = lax.rem(self.m, 4)
+        self.zl = lax.div(self.m, 4)
+
+    def chip(self, zl, x):
+        return 4 * zl + x
+
+    def at_chip(self, m):
+        return (2 * m + self.core, self.c)
+
+
+def remote(src, dst, send, recv, device):
+    return pltpu.make_async_remote_copy(
+        src_ref=src, dst_ref=dst, send_sem=send, recv_sem=recv, device_id=device, device_id_type=MESH
+    )
+
+
+class Spread:
+    def __init__(self, at, src, buf, sems, w):
+        self.at, self.src, self.buf, self.w = at, src, buf, w
+        (self.t_send, self.t_recv, self.z_send, self.z_recv, self.x_send, self.x_recv,
+         self.f_send, self.f_recv, self.d_send, self.d_recv, self.own_sem) = sems
+        self.rows = src.shape[1]
+        self.other = (at.r + 1 - 2 * at.core, at.c)
+        xl, xr = lax.rem(at.x + 3, 4), lax.rem(at.x + 1, 4)
+        self.xs = (xl, xr)
+        self.far = lax.rem(at.x + 2, 4)
+        self.zls = (at.zl, 1 - at.zl)
+
+    def block(self, m, core=None, tile=None):
+        core = self.at.core if core is None else core
+        rows = pl.ds(pl.multiple_of(m * self.rows, self.rows), self.rows)
+        if tile is None:
+            return self.buf.at[pl.ds(2 * core, 2), rows, :]
+        return self.buf.at[pl.ds(2 * core + tile, 1), rows, :]
+
+    def transpose_copy(self):
+        at = self.at
+        return remote(self.src, self.block(at.c), self.t_send.at[self.w], self.t_recv.at[self.w], (2 * at.c + at.core, at.m))
+
+    def transpose_local(self):
+        return pltpu.make_async_copy(self.src, self.block(self.at.c), self.own_sem.at[self.w])
+
+    def transpose_start(self):
+        @pl.when(self.at.m != self.at.c)
+        def _():
+            self.transpose_copy().start()
+
+        @pl.when(self.at.m == self.at.c)
+        def _():
+            self.transpose_local().start()
+
+    def transpose_wait(self):
+        at = self.at
+
+        @pl.when(at.m != at.c)
+        def _():
+            own = self.block(at.m)
+            remote(own, own, self.t_send.at[self.w], self.t_recv.at[self.w], (2 * at.c + at.core, at.m)).wait_recv()
+
+        @pl.when(at.m == at.c)
+        def _():
+            self.transpose_local().wait()
+
+    def z_copy(self, zl):
+        b = self.block(self.at.chip(zl, self.at.x))
+        return remote(b, b, self.z_send.at[self.w], self.z_recv.at[self.w], self.at.at_chip(self.at.chip(self.zls[1], self.at.x)))
+
+    def x_copy(self, s, to):
+        b = self.block(self.at.chip(self.zls[s], self.at.x))
+        return remote(b, b, self.x_send.at[self.w, s, to], self.x_recv.at[self.w, s, 1 - to], self.at.at_chip(self.at.chip(self.at.zl, self.xs[to])))
+
+    def x_wait(self, s, came):
+        b = self.block(self.at.chip(self.zls[s], self.xs[came]))
+        remote(b, b, self.x_send.at[self.w, s, came], self.x_recv.at[self.w, s, came], self.other).wait_recv()
+
+    def f_copy(self, s, came):
+        b = self.block(self.at.chip(self.zls[s], self.xs[came]), tile=came)
+        return remote(b, b, self.f_send.at[self.w, s, came], self.f_recv.at[self.w, s, came], self.at.at_chip(self.at.chip(self.at.zl, self.xs[1 - came])))
+
+    def f_wait(self, s, came):
+        b = self.block(self.at.chip(self.zls[s], self.far), tile=came)
+        remote(b, b, self.f_send.at[self.w, s, came], self.f_recv.at[self.w, s, came], self.other).wait_recv()
+
+    def d_copy(self, n, core=None):
+        at = self.at
+        core = at.core if core is None else core
+        if n < 2:
+            b = self.block(at.chip(self.zls[n], at.x), core)
+        elif n < 6:
+            s, came = divmod(n - 2, 2)
+            b = self.block(at.chip(self.zls[s], self.xs[came]), core)
+        else:
+            s, came = divmod(n - 6, 2)
+            b = self.block(at.chip(self.zls[s], self.far), core, came)
+        return remote(b, b, self.d_send.at[self.w, n], self.d_recv.at[self.w, n], self.other)
+
+    def stage_own(self):
+        self.transpose_wait()
+        self.x_copy(0, LEFT).start()
+        self.x_copy(0, RIGHT).start()
+        self.z_copy(self.zls[0]).start()
+        self.d_copy(0).start()
+
+    def stage_partner(self):
+        self.z_copy(self.zls[1]).wait_recv()
+        self.x_copy(1, LEFT).start()
+        self.x_copy(1, RIGHT).start()
+        self.d_copy(1).start()
+
+    def stage_forward(self, s):
+        for came in (LEFT, RIGHT):
+            self.x_wait(s, came)
+            self.f_copy(s, came).start()
+            self.d_copy(2 + 2 * s + came).start()
+
+    def stage_far(self, s):
+        for came in (LEFT, RIGHT):
+            self.f_wait(s, came)
+            self.d_copy(6 + 2 * s + came).start()
+
+    def stage_other_core(self):
+        for n in range(10):
+            self.d_copy(n, 1 - self.at.core).wait_recv()
+
+    def drain(self):
+        @pl.when(self.at.m != self.at.c)
+        def _():
+            self.transpose_copy().wait_send()
+
+        self.z_copy(self.zls[0]).wait_send()
+        for s in (0, 1):
+            for to in (LEFT, RIGHT):
+                self.x_copy(s, to).wait_send()
+                self.f_copy(s, to).wait_send()
+        for n in range(10):
+            self.d_copy(n).wait_send()
+
+
+def greet(at):
+    barrier = pltpu.get_barrier_semaphore()
+
+    def hello(device):
+        pl.semaphore_signal(barrier, inc=1, device_id=device, device_id_type=MESH)
+
+    for step in range(1, at.cols):
+        hello((at.r, lax.rem(at.c + step, at.cols)))
+    hello((at.r + 1 - 2 * at.core, at.c))
+    hello(at.at_chip(at.chip(1 - at.zl, at.x)))
+    hello(at.at_chip(at.chip(at.zl, lax.rem(at.x + 1, 4))))
+    hello(at.at_chip(at.chip(at.zl, lax.rem(at.x + 3, 4))))
+
+    @pl.when(at.m != at.c)
+    def _():
+        hello((2 * at.c + at.core, at.m))
+        pl.semaphore_wait(barrier, at.cols + 4)
+
+    @pl.when(at.m == at.c)
+    def _():
+        pl.semaphore_wait(barrier, at.cols + 3)
+
+
+class Group:
+    def __init__(self, at, send, recv):
+        self.at, self.send, self.recv = at, send, recv
+
+    def copy(self, src, dst, to):
+        return remote(src, dst, self.send.at[to], self.recv.at[self.at.c], (self.at.r, to))
+
+    def wait_from(self, dst, source):
+        remote(dst, dst, self.send.at[source], self.recv.at[source], (self.at.r, source)).wait_recv()
+
+
+def panel_kernel(rv_hbm, ru_hbm, cu_hbm, cv_hbm, d_hbm, cores_ref, r_hbm, c_hbm,
+                 vblk, rbuf, dbuf, dsp, yacc, zpart, zsend, zt, zsp, cub, cvb, csp,
+                 v_send, v_recv, r_send, r_recv, p_send, p_recv, q_send, q_recv,
+                 t_send, t_recv, z_send, z_recv, x_send, x_recv, f_send, f_recv, d_send, d_recv, own_sem, in_sem, out_sem):
+    cols, part, k = vblk.shape
+    rows = cols * part
+    at = Links(cols)
+    sems = (t_send, t_recv, z_send, z_recv, x_send, x_recv, f_send, f_recv, d_send, d_recv, own_sem)
+    cv = Spread(at, cv_hbm, cvb, sems, 0)
+    cu = Spread(at, cu_hbm, cub, sems, 1)
+    vg, rg, pg, qg = Group(at, v_send, v_recv), Group(at, r_send, r_recv), Group(at, p_send, p_recv), Group(at, q_send, q_recv)
+
+    def rblock(b):
+        return rbuf.at[pl.ds(pl.multiple_of(b * part, part), part), :]
+
+    def others(do, keep=None):
+        for step in range(1, cols):
+            b = lax.rem(at.c + step, cols)
+            if keep is None:
+                do(b)
+            else:
+                pl.when(keep(b))(lambda b=b: do(b))
+
+    later, earlier = (lambda b: b > at.c), (lambda b: b < at.c)
+    load_d = pltpu.make_async_copy(d_hbm, dbuf, in_sem.at[0])
+    load_v = pltpu.make_async_copy(rv_hbm.at[0], vblk.at[at.c], in_sem.at[1])
+    load_r = pltpu.make_async_copy(ru_hbm.at[0], rblock(at.c), in_sem.at[2])
+    load_d.start()
+    load_v.start()
+    load_r.start()
+    greet(at)
+    others(lambda b: vg.copy(rv_hbm.at[0], vblk.at[at.c], b).start(), later)
+    cv.transpose_start()
+    cu.transpose_start()
+    others(lambda b: rg.copy(ru_hbm.at[0], rblock(at.c), b).start())
+
+    load_d.wait()
+
+    def split_d(b, carry):
+        dsp[b] = halves(dbuf[:, pl.ds(pl.multiple_of(b * part, part), part)])
+        return carry
+
+    lax.fori_loop(0, at.c + 1, split_d, 0)
+    cv.stage_own()
+
+    def apply(b, first=False):
+        vs = halves(vblk[b])
+        q = dotb(dsp[b, :, :part], vs) + dotb(dsp[b, :, part:], vs)
+        yacc[...] = q if first else yacc[...] + q
+
+    load_v.wait()
+    apply(at.c, True)
+
+    def more(n, carry):
+        b = at.c - 1 - n
+        vg.wait_from(vblk.at[b], b)
+        apply(b)
+        return carry
+
+    lax.fori_loop(0, at.c, more, 0)
+    y = yacc[:, :k] + yacc[:, k:]
+    yt = halves(y).astype(f32).T.astype(bf16)
+
+    def back(b):
+        q = dotb(yt, dsp[b])
+        q = q[:k] + q[k:]
+        return q[:, :part] + q[:, part:]
+
+    def send_back(n, carry):
+        zsend[n] = back(n)
+        pg.copy(zsend.at[n], zpart.at[at.c], n).start()
+        return carry
+
+    lax.fori_loop(0, at.c, send_back, 0)
+    cv.stage_partner()
+    zt[at.c] = back(at.c)
+    cv.stage_forward(0)
+
+    def gather(n, carry):
+        b = cols - 1 - n
+        pg.wait_from(zpart.at[b], b)
+        zt[at.c] = zt[at.c] + zpart[b]
+        return carry
+
+    lax.fori_loop(0, cols - 1 - at.c, gather, 0)
+    others(lambda b: qg.copy(zt.at[at.c], zt.at[at.c], b).start())
+    cv.stage_forward(1)
+    cu.stage_own()
+    cv.stage_far(0)
+    cv.stage_far(1)
+    cu.stage_partner()
+    others(lambda b: qg.wait_from(zt.at[b], b))
+    for b in range(cols):
+        z = zt[b]
+        hi = z.astype(bf16)
+        zsp[:k, part * b : part * (b + 1)] = hi
+        zsp[k:, part * b : part * (b + 1)] = (z - hi.astype(f32)).astype(bf16)
+    cu.stage_forward(0)
+    cv.stage_other_core()
+    for t in range(cores_ref.shape[0]):
+
+        def split_c(n, carry, t=t):
+            ds = pl.ds(pl.multiple_of(n * part, part), part)
+            csp[ds, :] = halves(cvb[t, ds, :])
+            return carry
+
+        lax.fori_loop(0, cols, split_c, 0)
+        cores_ref[t] = fold4(dotb(zsp[...], csp[...]))
+        if t == 0:
+            cu.stage_forward(1)
+    cu.stage_far(0)
+    cu.stage_far(1)
+    load_r.wait()
+    others(lambda b: rg.wait_from(rblock(b), b))
+    out_r = pltpu.make_async_copy(rbuf, r_hbm, out_sem.at[0])
+    out_r.start()
+    cu.stage_other_core()
+    out_c = pltpu.make_async_copy(cub, c_hbm, out_sem.at[1])
+    out_c.start()
+
+    others(lambda b: vg.copy(rv_hbm.at[0], vblk.at[at.c], b).wait_send(), later)
+    others(lambda b: rg.copy(ru_hbm.at[0], rblock(at.c), b).wait_send())
+    others(lambda b: pg.copy(zsend.at[b], zpart.at[at.c], b).wait_send(), earlier)
+    others(lambda b: qg.copy(zt.at[at.c], zt.at[at.c], b).wait_send())
+    cv.drain()
+    cu.drain()
+    out_r.wait()
+    out_c.wait()
+
+
+def spread_panels(row_v, row_u, col_u, col_v, diag, tiles):
+    cols = lax.axis_size("col")
+    part, k = row_v.shape[1:]
+    rows = cols * part
+    vm = pl.BlockSpec(memory_space=pltpu.VMEM)
+    hbm = pl.BlockSpec(memory_space=pl.ANY)
+    dma = pltpu.SemaphoreType.DMA
+    return pl.pallas_call(
+        panel_kernel,
+        name="spread_panels",
+        out_shape=(
+            jax.ShapeDtypeStruct((tiles, k, k), f32),
+            jax.ShapeDtypeStruct((rows, k), f32),
+            jax.ShapeDtypeStruct((tiles, rows, k), f32),
+        ),
+        in_specs=[hbm] * 5,
+        out_specs=(vm, hbm, hbm),
+        scratch_shapes=[
+            pltpu.VMEM((cols, part, k), f32),
+            pltpu.VMEM((rows, k), f32),
+            pltpu.VMEM((part, rows), f32),
+            pltpu.VMEM((cols, part, 2 * part), bf16),
+            pltpu.VMEM((part, 2 * k), f32),
+            pltpu.VMEM((cols, k, part), f32),
+            pltpu.VMEM((cols, k, part), f32),
+            pltpu.VMEM((cols, k, part), f32),
+            pltpu.VMEM((2 * k, rows), bf16),
+            pltpu.VMEM((tiles, rows, k), f32),
+            pltpu.VMEM((tiles, rows, k), f32),
+            pltpu.VMEM((rows, 2 * k), bf16),
+        ]
+        + [dma((cols,))] * 8
+        + [dma((2,))] * 4
+        + [dma((2, 2, 2))] * 4
+        + [dma((2, 10))] * 2
+        + [dma((2,)), dma((3,)), dma((2,))],
+        compiler_params=pltpu.CompilerParams(collective_id=0, has_side_effects=True, vmem_limit_bytes=50 * 2**20),
+        cost_estimate=pl.CostEstimate(flops=10**9, bytes_accessed=16 * 2**20, transcendentals=0),
+    )(row_v, row_u, col_u, col_v, diag)
 
 
 def body(tile_u, tile_v, row_panel_u, row_panel_v, col_panel_u, col_panel_v, diag_inverse, sketch):
-    pieces = side_by_side((row_panel_v, col_panel_v), "col", 1, 0)
-    first = jnp.einsum("ab,tbk->tak", diag_inverse, pieces[0], precision=highest)
-    second = jnp.einsum("ab,tbk->tak", diag_inverse, pieces[1], precision=highest)
-    col_u_rows, col_v_rows = side_by_side((col_panel_u, second), "row", 0, 1)
-    row_u_full = gather_directly(row_panel_u, "col", 1)
-    col_u_full = lax.all_to_all(col_u_rows, "col", split_axis=0, concat_axis=1, tiled=True)
-    partial_cores = jnp.einsum("iak,jal->ijkl", first, col_v_rows, precision=highest)
-    cores = sum_at_owner(partial_cores, "col", 1)
-    new_u, new_v = recompress(tile_u[0], tile_v[0], row_u_full[0], col_u_full, cores[0], sketch)
+    cores, row_u, col_u = spread_panels(row_panel_v, row_panel_u, col_panel_u, col_panel_v, diag_inverse, tile_u.shape[1])
+    new_u, new_v = recompress(tile_u[0], tile_v[0], row_u, col_u, cores, sketch)
     return new_u[None], new_v[None]
 
 

time: 305 us -> 142 us (0.47)
  waiting for transfers between devices: 151 us -> 0 us
  Pallas kernels: 36.7 us -> 136 us
  blocking collectives: 53.2 us -> 0 us
  matrix products: 17.1 us -> 0 us
  between operations: 14.1 us -> 0.82 us
  local copies, waits for them, and re-layouts: 16.9 us -> 4.92 us
  starting transfers between devices: 10.2 us -> 0 us
  other arithmetic: 3.25 us -> 0 us
    all_gather x2 -> x0, waiting for transfers between devices: 118 us -> none  [side_by_side(): filled = lax.all_gather(both, axis, axis=dim, tiled=True)]
    pallas_call x0 -> x1, Pallas kernels: none -> 99.5 us  [spread_panels(): pl.pallas_call(panel_kernel, name='spread_panels', out_shape=(jax.ShapeDt...]
    all_to_all x1 -> x0, blocking collectives: 53.2 us -> none  [body(): lax.all_to_all(col_u_rows, 'col', split_axis=0, concat_axis=1, tiled=True)]
    all_to_all x2 -> x0, waiting for transfers between devices: 32.1 us -> none  [the longest x1 26.4 us: sum_at_owner(): lax.all_to_all(parts, axis, split_axis=0, concat_axis=0, tiled=True)]
    dot_general x3 -> x0, matrix products: 17.1 us -> none  [the longest x1 10.2 us: body(): jnp.einsum('iak,jal->ijkl', first, col_v_rows, precision=highest)]
    all_to_all x2 -> x0, starting transfers between devices: 10.2 us -> none  [the longest x1 6.42 us: sum_at_owner(): lax.all_to_all(parts, axis, split_axis=0, concat_axis=0, tiled=True)]
    split x1 -> x0, local copies, waits for them, and re-layouts: 4.66 us -> none  [side_by_side(): jnp.split(filled, [sum(widths[:k]) for k in range(1, len(widths))], axis=...]
    all_to_all x1 -> x0, local copies, waits for them, and re-layouts: 4.61 us -> none  [body(): lax.all_to_all(col_u_rows, 'col', split_axis=0, concat_axis=1, tiled=True)]
  transfers between devices with their start and end apart: 4 -> 0, of which waited for: 4 -> 0; matrix products, arithmetic and copies ran while one was open for 6% -> 0% of each run, Pallas kernels for 0% -> 0%
where the time goes in v1:
time: 142 us
  Pallas kernels  136 us (96%)
  local copies, waits for them, and re-layouts  4.92 us (3%)
    pallas_call x1, Pallas kernels, spread_panels(): pl.pallas_call(panel_kernel, name='spread_panels', out_shape=(jax.ShapeDt...  99.5 us
    pallas_call x1, Pallas kernels, recompress(): pl.pallas_call(local_kernel, name='recompress', out_shape=(out, out), in_...  36.9 us
    unnamed x10, local copies, waits for them, and re-layouts  4.92 us

profile of v1, /device:TPU:1, one launch (start us, length us, event | category | flops | bytes accessed | tf_op | source)
XLA Modules:
  0.0 142.1 jit_solution(4762307454890128094)
XLA Ops:
  0.6 0.0 copy-start.1
  0.6 0.9 copy-done.1
  1.6 0.0 copy-start.2
  1.6 0.9 copy-done.2
  2.5 0.0 copy-start.3
  2.5 0.9 copy-done.3
  3.4 0.0 copy-start.4
  3.4 0.9 copy-done.4
  4.3 99.5 %spread_panels.1 = (f32[4,128,128]{2,1,0:T(8,128)S(1)}, f32[2048,128]{1,0:T(8,128)S(1)}, f32[4,2048,128]{2,1,0:T(8,128)}) custom-call(f32[1,256,128]{2,1,0:T(8,128)S(1)} %copy-done.3, f32[1,256,128]{2,1,0:T(8,128)S(1)} %copy-done.4, f32[2,256,128]{2,1,0:T(8,128)S(1)} %copy-done.1, f32[2,256,128]{2,1,0:T(8,128)S(1)} %copy-done.2, f32[256,2048]{1,0:T(8,128)} %d_hbm.1), custom_call_target="tpu_custom_call" | custom-call | flops 1000000000 | bytes 16777216 | tf_op jit(solution)/shard_map/spread_panels/pallas_call | solution.py:507
  103.8 0.0 copy-start
  103.8 1.2 copy-done
  105.0 36.9 %recompress.1 = (f32[4,2048,128]{2,1,0:T(8,128)}, f32[4,2048,128]{2,1,0:T(8,128)}) custom-call(f32[4,2048,128]{2,1,0:T(8,128)} %bitcast.4, f32[4,2048,128]{2,1,0:T(8,128)} %bitcast.5, f32[2048,128]{1,0:T(8,128)S(1)} %get-tuple-element.7.r_ref, f32[4,2048,128]{2,1,0:T(8,128)} %get-tuple-element.8.c_hbm, f32[4,128,128]{2,1,0:T(8,128)S(1)} %get-tuple-element.9.cores_ref, ...), custom_call_target="tpu_custom_call" | custom-call | flops 10000000000 | bytes 25165824 | tf_op jit(solution)/shard_map/recompress/pallas_call | solution.py:159
Async XLA Ops:
  0.6 1.0 copy-start.1
  1.6 0.9 copy-start.2
  2.5 0.9 copy-start.3
  3.4 0.9 copy-start.4
  103.8 1.2 copy-start

commit v2 on v1

--- a/solution.py
+++ b/solution.py
@@ -74,8 +74,8 @@
                     inv_ref[t, lo + 8 :, :] = inv_ref[t, lo + 8 :, :] - upd[lo + 8 :, k:]
 
 
-def local_kernel(u_hbm, v_hbm, r_ref, c_hbm, cores_ref, s_ref, nu_hbm, nv_hbm,
-                 ubuf, vbuf, cbuf, usp, vsp, csp, rsp, tt, w_s, t_s, gram_s, inv_s, fac_s, in_sem, out_sem):
+def finish_kernel(u_hbm, v_hbm, r_hbm, c_hbm, cores_hbm, w_hbm, t_hbm, gram_hbm, nu_hbm, nv_hbm,
+                  ubuf, vbuf, cbuf, rbuf, cores_ref, w_ref, t_ref, gram_s, inv_s, fac_s, in_sem, r_sem, out_sem):
     tiles, rows, k = ubuf.shape
     step = min(512, rows)
     scaling = math.sqrt(rows)
@@ -84,62 +84,39 @@
         src, dst = ((u_hbm, ubuf), (v_hbm, vbuf), (c_hbm, cbuf))[which]
         return pltpu.make_async_copy(src.at[t], dst.at[t], in_sem.at[which, t])
 
+    singles = [
+        pltpu.make_async_copy(src, dst, r_sem.at[n])
+        for n, (src, dst) in enumerate(((gram_hbm, gram_s), (w_hbm, w_ref), (t_hbm, t_ref), (cores_hbm, cores_ref), (r_hbm, rbuf)))
+    ]
+    for copy in singles:
+        copy.start()
     for t in range(tiles):
         for which in range(3):
             load(t, which).start()
-
-    for lo in range(0, rows, step):
-        for n, ref in enumerate((r_ref, s_ref)):
-            h = halves(ref[lo : lo + step, :])
-            if n == 0:
-                rsp[lo : lo + step, :] = h
-            tt[n, :, lo : lo + step] = h.astype(f32).T.astype(bf16)
-    rr = fold4(dotb(tt[0], rsp[...]))
-
+    singles[0].wait()
+    inverse_factors(gram_s, inv_s, fac_s)
+
+    def store(t, which):
+        src, dst = ((ubuf, nu_hbm), (vbuf, nv_hbm))[which]
+        return pltpu.make_async_copy(src.at[t], dst.at[t], out_sem.at[which, t])
+
+    for copy in singles[1:]:
+        copy.wait()
     for t in range(tiles):
         for which in range(3):
             load(t, which).wait()
-            buf, sp = ((ubuf, usp), (vbuf, vsp), (cbuf, csp))[which]
-
-            def body(n, carry, buf=buf, sp=sp, t=t):
-                at = pl.ds(pl.multiple_of(n * step, step), step)
-                sp[t, at, :] = halves(buf[t, at, :])
-                return carry
-
-            lax.fori_loop(0, rows // step, body, 0)
-        uu = fold4(dotb(usp[t], usp[t], 0, 0))
-        ru = fold4(dotb(tt[0], usp[t]))
-        p1t = fold4(dotb(tt[1], vsp[t]))
-        p2t = fold4(dotb(tt[1], csp[t]))
-        cores = cores_ref[t]
-        w1 = p1t.T
-        w2 = -dot(cores, p2t, 1, 1)
-        w = jnp.concatenate([w1, w2], axis=0)
-        g = jnp.concatenate([jnp.concatenate([uu, ru.T], axis=1), jnp.concatenate([ru, rr], axis=1)], axis=0)
-        tw = dot(g, w)
-        w_s[t] = w
-        t_s[t] = tw
-        gram_s[t] = dot(w, tw, 0, 0)
-
-    inverse_factors(gram_s, inv_s, fac_s)
-
-    def store(t, which):
-        src, dst = ((ubuf, nu_hbm), (vbuf, nv_hbm))[which]
-        return pltpu.make_async_copy(src.at[t], dst.at[t], out_sem.at[which, t])
-
-    for t in range(tiles):
         fac = fac_s[t]
-        x = dot(w_s[t], fac, 1, 1) * scaling
-        y = dot(t_s[t], fac, 1, 1) * (1.0 / scaling)
+        x = dot(w_ref[t], fac, 1, 1) * scaling
+        y = dot(t_ref[t], fac, 1, 1) * (1.0 / scaling)
         c1 = y[:k]
         c2 = -dot(cores_ref[t], y[k:], 0, 0)
         x1, x2, c1, c2 = doubled(x[:k]), doubled(x[k:]), doubled(c1), doubled(c2)
 
         def finish(n, carry, t=t, x1=x1, x2=x2, c1=c1, c2=c2):
             at = pl.ds(pl.multiple_of(n * step, step), step)
-            a = dotb(usp[t, at, :], x1) + dotb(rsp[at, :], x2)
+            a = dotb(halves(ubuf[t, at, :]), x1) + dotb(halves(rbuf[at, :]), x2)
             ubuf[t, at, :] = a[:, :k] + a[:, k:]
-            b = dotb(vsp[t, at, :], c1) + dotb(csp[t, at, :], c2)
+            b = dotb(halves(vbuf[t, at, :]), c1) + dotb(halves(cbuf[t, at, :]), c2)
             vbuf[t, at, :] = b[:, :k] + b[:, k:]
             return carry
 
@@ -151,41 +128,45 @@
         store(t, 1).wait()
 
 
-def recompress(tile_u, tile_v, row_u, col_u, cores, sketch):
+def recompress(tile_u, tile_v, row_u, col_u, cores, w, tw, gram):
     tiles, rows, k = tile_u.shape
-    vm = pl.BlockSpec(memory_space=pltpu.VMEM)
-    hbm = pl.BlockSpec(memory_space=pl.ANY)
+    hbm = pl.BlockSpec(memory_space=pltpu.HBM)
     out = jax.ShapeDtypeStruct(tile_u.shape, f32)
     return pl.pallas_call(
-        local_kernel,
+        finish_kernel,
         name="recompress",
         out_shape=(out, out),
-        in_specs=[hbm, hbm, vm, hbm, vm, vm],
+        in_specs=[hbm] * 8,
         out_specs=(hbm, hbm),
         scratch_shapes=[
             pltpu.VMEM((tiles, rows, k), f32),
             pltpu.VMEM((tiles, rows, k), f32),
             pltpu.VMEM((tiles, rows, k), f32),
-            pltpu.VMEM((tiles, rows, 2 * k), bf16),
-            pltpu.VMEM((tiles, rows, 2 * k), bf16),
-            pltpu.VMEM((tiles, rows, 2 * k), bf16),
-            pltpu.VMEM((rows, 2 * k), bf16),
-            pltpu.VMEM((2, 2 * k, rows), bf16),
+            pltpu.VMEM((rows, k), f32),
+            pltpu.VMEM((tiles, k, k), f32),
             pltpu.VMEM((tiles, 2 * k, k), f32),
             pltpu.VMEM((tiles, 2 * k, k), f32),
             pltpu.VMEM((tiles, k, k), f32),
             pltpu.VMEM((tiles, k, k), f32),
             pltpu.VMEM((tiles, k, k), f32),
             pltpu.SemaphoreType.DMA((3, tiles)),
+            pltpu.SemaphoreType.DMA((5,)),
             pltpu.SemaphoreType.DMA((2, tiles)),
         ],
-        compiler_params=pltpu.CompilerParams(vmem_limit_bytes=50 * 2**20),
+        compiler_params=pltpu.CompilerParams(vmem_limit_bytes=60 * 2**20),
         cost_estimate=pl.CostEstimate(flops=10**10, bytes_accessed=24 * 2**20, transcendentals=0),
-    )(tile_u, tile_v, row_u, col_u, cores, sketch)
+    )(tile_u, tile_v, row_u, col_u, cores, w, tw, gram)
 
 
 MESH = pl.DeviceIdType.MESH
 CENTRE, ACROSS, LEFT, RIGHT = 0, 1, 0, 1
+
+
+def mix(a, b):
+    out = 0
+    for bit in (4, 2, 1):
+        out = out + bit * lax.rem(lax.div(a, bit) + lax.div(b, bit), 2)
+    return out
 
 
 class Links:
@@ -197,6 +178,10 @@
         self.m = lax.div(self.r, 2)
         self.x = lax.rem(self.m, 4)
         self.zl = lax.div(self.m, 4)
+        self.mixed = mix(self.m, self.c)
+        self.target = (2 * self.mixed + self.core, self.m)
+        self.source = (2 * self.c + self.core, self.mixed)
+        self.alone = jnp.logical_and(self.m == 0, self.c == 0)
 
     def chip(self, zl, x):
         return 4 * zl + x
@@ -225,36 +210,38 @@
 
     def block(self, m, core=None, tile=None):
         core = self.at.core if core is None else core
-        rows = pl.ds(pl.multiple_of(m * self.rows, self.rows), self.rows)
+        rows = pl.ds(pl.multiple_of(mix(m, self.at.c) * self.rows, self.rows), self.rows)
         if tile is None:
             return self.buf.at[pl.ds(2 * core, 2), rows, :]
         return self.buf.at[pl.ds(2 * core + tile, 1), rows, :]
 
     def transpose_copy(self):
         at = self.at
-        return remote(self.src, self.block(at.c), self.t_send.at[self.w], self.t_recv.at[self.w], (2 * at.c + at.core, at.m))
+        rows = pl.ds(pl.multiple_of(at.c * self.rows, self.rows), self.rows)
+        dst = self.buf.at[pl.ds(2 * at.core, 2), rows, :]
+        return remote(self.src, dst, self.t_send.at[self.w], self.t_recv.at[self.w], at.target)
 
     def transpose_local(self):
-        return pltpu.make_async_copy(self.src, self.block(self.at.c), self.own_sem.at[self.w])
+        return pltpu.make_async_copy(self.src, self.block(self.at.m), self.own_sem.at[self.w])
 
     def transpose_start(self):
-        @pl.when(self.at.m != self.at.c)
+        @pl.when(jnp.logical_not(self.at.alone))
         def _():
             self.transpose_copy().start()
 
-        @pl.when(self.at.m == self.at.c)
+        @pl.when(self.at.alone)
         def _():
             self.transpose_local().start()
 
     def transpose_wait(self):
         at = self.at
 
-        @pl.when(at.m != at.c)
+        @pl.when(jnp.logical_not(at.alone))
         def _():
             own = self.block(at.m)
-            remote(own, own, self.t_send.at[self.w], self.t_recv.at[self.w], (2 * at.c + at.core, at.m)).wait_recv()
-
-        @pl.when(at.m == at.c)
+            remote(own, own, self.t_send.at[self.w], self.t_recv.at[self.w], at.source).wait_recv()
+
+        @pl.when(at.alone)
         def _():
             self.transpose_local().wait()
 
@@ -320,7 +307,7 @@
             self.d_copy(n, 1 - self.at.core).wait_recv()
 
     def drain(self):
-        @pl.when(self.at.m != self.at.c)
+        @pl.when(jnp.logical_not(self.at.alone))
         def _():
             self.transpose_copy().wait_send()
 
@@ -346,12 +333,13 @@
     hello(at.at_chip(at.chip(at.zl, lax.rem(at.x + 1, 4))))
     hello(at.at_chip(at.chip(at.zl, lax.rem(at.x + 3, 4))))
 
-    @pl.when(at.m != at.c)
+    @pl.when(jnp.logical_not(at.alone))
     def _():
-        hello((2 * at.c + at.core, at.m))
-        pl.semaphore_wait(barrier, at.cols + 4)
-
-    @pl.when(at.m == at.c)
+        hello(at.target)
+        hello(at.source)
+        pl.semaphore_wait(barrier, at.cols + 5)
+
+    @pl.when(at.alone)
     def _():
         pl.semaphore_wait(barrier, at.cols + 3)
 
@@ -367,20 +355,96 @@
         remote(dst, dst, self.send.at[source], self.recv.at[source], (self.at.r, source)).wait_recv()
 
 
-def panel_kernel(rv_hbm, ru_hbm, cu_hbm, cv_hbm, d_hbm, cores_ref, r_hbm, c_hbm,
-                 vblk, rbuf, dbuf, dsp, yacc, zpart, zsend, zt, zsp, cub, cvb, csp,
-                 v_send, v_recv, r_send, r_recv, p_send, p_recv, q_send, q_recv,
-                 t_send, t_recv, z_send, z_recv, x_send, x_recv, f_send, f_recv, d_send, d_recv, own_sem, in_sem, out_sem):
+class Tree:
+    def __init__(self, at, block, sems):
+        self.at, self.block = at, block
+        self.z_send, self.z_recv, self.y_send, self.y_recv, self.f_send, self.f_recv = sems
+        y, zh = lax.div(at.c, 2), lax.rem(at.c, 2)
+        self.zhs = (zh, 1 - zh)
+        self.ys = (lax.rem(y + 3, 4), lax.rem(y + 1, 4))
+        self.y, self.far = y, lax.rem(y + 2, 4)
+
+    def col(self, y, s):
+        return 2 * y + self.zhs[s]
+
+    def z_copy(self, s):
+        b = self.block(self.col(self.y, s))
+        return remote(b, b, self.z_send.at[0], self.z_recv.at[0], (self.at.r, self.col(self.y, 1)))
+
+    def y_copy(self, s, to):
+        b = self.block(self.col(self.y, s))
+        return remote(b, b, self.y_send.at[s, to], self.y_recv.at[s, 1 - to], (self.at.r, self.col(self.ys[to], 0)))
+
+    def y_wait(self, s, came):
+        b = self.block(self.col(self.ys[came], s))
+        remote(b, b, self.y_send.at[s, came], self.y_recv.at[s, came], (self.at.r, self.col(self.ys[came], 0))).wait_recv()
+
+    def f_copy(self, s, came):
+        b = self.block(self.col(self.ys[came], s), came)
+        return remote(b, b, self.f_send.at[s, came], self.f_recv.at[s, came], (self.at.r, self.col(self.ys[1 - came], 0)))
+
+    def f_wait(self, s, came):
+        b = self.block(self.col(self.far, s), came)
+        remote(b, b, self.f_send.at[s, came], self.f_recv.at[s, came], (self.at.r, self.col(self.ys[came], 0))).wait_recv()
+
+    def stage_own(self):
+        self.z_copy(0).start()
+        self.y_copy(0, LEFT).start()
+        self.y_copy(0, RIGHT).start()
+
+    def stage_partner(self):
+        self.z_copy(1).wait_recv()
+        self.y_copy(1, LEFT).start()
+        self.y_copy(1, RIGHT).start()
+
+    def stage_forward(self, s):
+        for came in (LEFT, RIGHT):
+            self.y_wait(s, came)
+            self.f_copy(s, came).start()
+
+    def stage_far(self, s):
+        for came in (LEFT, RIGHT):
+            self.f_wait(s, came)
+
+    def drain(self):
+        self.z_copy(0).wait_send()
+        for s in (0, 1):
+            for to in (LEFT, RIGHT):
+                self.y_copy(s, to).wait_send()
+                self.f_copy(s, to).wait_send()
+
+
+def panel_kernel(rv_hbm, ru_hbm, cu_hbm, cv_hbm, d_hbm, u_hbm, v_hbm, s_ref, w_ref, t_ref, gram_ref, cores_ref, r_hbm, c_hbm,
+                 vblk, vsp, rbuf, rsp, dbuf, dsp, zpart, zsend, zt, zsp, cub, cvb, csp, ubuf, vbuf, usp, tts, ttr, uu_s, p1_s, ru_s,
+                 v_send, v_recv, p_send, p_recv, rz_send, rz_recv, ry_send, ry_recv, rf_send, rf_recv,
+                 qz_send, qz_recv, qy_send, qy_recv, qf_send, qf_recv,
+                 t_send, t_recv, z_send, z_recv, x_send, x_recv, f_send, f_recv, d_send, d_recv, own_sem, in_sem, out_sem, uv_sem):
     cols, part, k = vblk.shape
+    tiles = ubuf.shape[0]
     rows = cols * part
     at = Links(cols)
     sems = (t_send, t_recv, z_send, z_recv, x_send, x_recv, f_send, f_recv, d_send, d_recv, own_sem)
     cv = Spread(at, cv_hbm, cvb, sems, 0)
     cu = Spread(at, cu_hbm, cub, sems, 1)
-    vg, rg, pg, qg = Group(at, v_send, v_recv), Group(at, r_send, r_recv), Group(at, p_send, p_recv), Group(at, q_send, q_recv)
-
-    def rblock(b):
-        return rbuf.at[pl.ds(pl.multiple_of(b * part, part), part), :]
+    vg, pg = Group(at, v_send, v_recv), Group(at, p_send, p_recv)
+
+    def span(b):
+        return pl.ds(pl.multiple_of(b * part, part), part)
+
+    def rblock(b, half=None):
+        if half is None:
+            return rbuf.at[span(b), :]
+        size = part // 2
+        return rbuf.at[pl.ds(pl.multiple_of(b * part + half * size, size), size), :]
+
+    def zblock(b, half=None):
+        if half is None:
+            return zt.at[b]
+        size = k // 2
+        return zt.at[b, size * half : size * (half + 1), :]
+
+    rg = Tree(at, rblock, (rz_send, rz_recv, ry_send, ry_recv, rf_send, rf_recv))
+    qg = Tree(at, zblock, (qz_send, qz_recv, qy_send, qy_recv, qf_send, qf_recv))
 
     def others(do, keep=None):
         for step in range(1, cols):
@@ -388,12 +452,20 @@
             if keep is None:
                 do(b)
             else:
-                pl.when(keep(b))(lambda b=b: do(b))
+
+                @pl.when(keep(b))
+                def _(b=b):
+                    do(b)
 
     later, earlier = (lambda b: b > at.c), (lambda b: b < at.c)
     load_d = pltpu.make_async_copy(d_hbm, dbuf, in_sem.at[0])
     load_v = pltpu.make_async_copy(rv_hbm.at[0], vblk.at[at.c], in_sem.at[1])
     load_r = pltpu.make_async_copy(ru_hbm.at[0], rblock(at.c), in_sem.at[2])
+
+    def load_tile(t, which):
+        src, dst = ((u_hbm, ubuf), (v_hbm, vbuf))[which]
+        return pltpu.make_async_copy(src.at[t], dst.at[t], uv_sem.at[which, t])
+
     load_d.start()
     load_v.start()
     load_r.start()
@@ -401,49 +473,73 @@
     others(lambda b: vg.copy(rv_hbm.at[0], vblk.at[at.c], b).start(), later)
     cv.transpose_start()
     cu.transpose_start()
-    others(lambda b: rg.copy(ru_hbm.at[0], rblock(at.c), b).start())
+    for t in range(tiles):
+        load_tile(t, 0).start()
+        load_tile(t, 1).start()
+
+    for b in range(cols):
+
+        @pl.when(b > at.c)
+        def _(b=b):
+            vsp[part * b : part * (b + 1), :] = jnp.zeros((part, 2 * k), bf16)
 
     load_d.wait()
 
     def split_d(b, carry):
-        dsp[b] = halves(dbuf[:, pl.ds(pl.multiple_of(b * part, part), part)])
+        d = dbuf[:, span(b)]
+        hi = d.astype(bf16)
+        dsp[0, :, span(b)] = hi
+        dsp[1, :, span(b)] = (d - hi.astype(f32)).astype(bf16)
         return carry
 
-    lax.fori_loop(0, at.c + 1, split_d, 0)
+    lax.fori_loop(0, cols, split_d, 0)
+
+    def split_s(b, carry):
+        tts[:, span(b)] = halves(s_ref[span(b), :]).astype(f32).T.astype(bf16)
+        return carry
+
+    lax.fori_loop(0, cols, split_s, 0)
+
+    def split_into(dst, src):
+        def body(b, carry):
+            dst[span(b), :] = halves(src[span(b), :])
+            return carry
+
+        lax.fori_loop(0, cols, body, 0)
+
+    def tile_products(t):
+        load_tile(t, 0).wait()
+        load_tile(t, 1).wait()
+        split_into(usp.at[t], ubuf.at[t])
+        uu_s[t] = fold4(dotb(usp[t], usp[t], 0, 0))
+        split_into(csp, vbuf.at[t])
+        p1_s[t] = fold4(dotb(tts[...], csp[...]))
+
     cv.stage_own()
-
-    def apply(b, first=False):
-        vs = halves(vblk[b])
-        q = dotb(dsp[b, :, :part], vs) + dotb(dsp[b, :, part:], vs)
-        yacc[...] = q if first else yacc[...] + q
-
+    cu.stage_own()
     load_v.wait()
-    apply(at.c, True)
-
-    def more(n, carry):
-        b = at.c - 1 - n
+    vsp[span(at.c), :] = halves(vblk[at.c])
+
+    def arrived(b, carry):
         vg.wait_from(vblk.at[b], b)
-        apply(b)
+        vsp[span(b), :] = halves(vblk[b])
         return carry
 
-    lax.fori_loop(0, at.c, more, 0)
-    y = yacc[:, :k] + yacc[:, k:]
-    yt = halves(y).astype(f32).T.astype(bf16)
-
-    def back(b):
-        q = dotb(yt, dsp[b])
-        q = q[:k] + q[k:]
-        return q[:, :part] + q[:, part:]
-
-    def send_back(n, carry):
-        zsend[n] = back(n)
-        pg.copy(zsend.at[n], zpart.at[at.c], n).start()
-        return carry
-
-    lax.fori_loop(0, at.c, send_back, 0)
+    lax.fori_loop(0, at.c, arrived, 0)
+    q = dotb(dsp[0], vsp[...]) + dotb(dsp[1], vsp[...])
+    yt = halves(q[:, :k] + q[:, k:]).astype(f32).T.astype(bf16)
+    for b in range(cols):
+        q = dotb(yt, dsp[0, :, part * b : part * (b + 1)]) + dotb(yt, dsp[1, :, part * b : part * (b + 1)])
+        zsend[b] = q[:k] + q[k:]
+    others(lambda b: pg.copy(zsend.at[b], zpart.at[at.c], b).start(), earlier)
     cv.stage_partner()
-    zt[at.c] = back(at.c)
+    cu.stage_partner()
+    load_r.wait()
+    rg.stage_own()
+    tile_products(0)
     cv.stage_forward(0)
+    cu.stage_forward(0)
+    zt[at.c] = zsend[at.c]
 
     def gather(n, carry):
         b = cols - 1 - n
@@ -452,74 +548,102 @@
         return carry
 
     lax.fori_loop(0, cols - 1 - at.c, gather, 0)
-    others(lambda b: qg.copy(zt.at[at.c], zt.at[at.c], b).start())
+    qg.stage_own()
+    rg.stage_partner()
+    tile_products(1)
+    qg.stage_partner()
     cv.stage_forward(1)
-    cu.stage_own()
+    cu.stage_forward(1)
+    rg.stage_forward(0)
+    qg.stage_forward(0)
+    tile_products(2)
+    rg.stage_forward(1)
+    qg.stage_forward(1)
+    tile_products(3)
     cv.stage_far(0)
+    cu.stage_far(0)
     cv.stage_far(1)
-    cu.stage_partner()
-    others(lambda b: qg.wait_from(zt.at[b], b))
+    cu.stage_far(1)
+    rg.stage_far(0)
+    rg.stage_far(1)
+    out_r = pltpu.make_async_copy(rbuf, r_hbm, out_sem.at[0])
+    out_r.start()
+
+    def split_r(b, carry):
+        h = halves(rbuf[span(b), :])
+        rsp[span(b), :] = h
+        ttr[:, span(b)] = h.astype(f32).T.astype(bf16)
+        return carry
+
+    lax.fori_loop(0, cols, split_r, 0)
+    rr = fold4(dotb(ttr[...], rsp[...]))
+    for t in range(tiles):
+        ru_s[t] = fold4(dotb(ttr[...], usp[t]))
+    qg.stage_far(0)
+    qg.stage_far(1)
     for b in range(cols):
         z = zt[b]
         hi = z.astype(bf16)
         zsp[:k, part * b : part * (b + 1)] = hi
         zsp[k:, part * b : part * (b + 1)] = (z - hi.astype(f32)).astype(bf16)
-    cu.stage_forward(0)
     cv.stage_other_core()
-    for t in range(cores_ref.shape[0]):
-
-        def split_c(n, carry, t=t):
-            ds = pl.ds(pl.multiple_of(n * part, part), part)
-            csp[ds, :] = halves(cvb[t, ds, :])
-            return carry
-
-        lax.fori_loop(0, cols, split_c, 0)
+    for t in range(tiles):
+        split_into(csp, cvb.at[t])
         cores_ref[t] = fold4(dotb(zsp[...], csp[...]))
-        if t == 0:
-            cu.stage_forward(1)
-    cu.stage_far(0)
-    cu.stage_far(1)
-    load_r.wait()
-    others(lambda b: rg.wait_from(rblock(b), b))
-    out_r = pltpu.make_async_copy(rbuf, r_hbm, out_sem.at[0])
-    out_r.start()
     cu.stage_other_core()
     out_c = pltpu.make_async_copy(cub, c_hbm, out_sem.at[1])
     out_c.start()
+    for t in range(tiles):
+        split_into(csp, cub.at[t])
+        p2t = fold4(dotb(tts[...], csp[...]))
+        w1 = p1_s[t].T
+        w2 = -dot(cores_ref[t], p2t, 1, 1)
+        w = jnp.concatenate([w1, w2], axis=0)
+        ru = ru_s[t]
+        g = jnp.concatenate([jnp.concatenate([uu_s[t], ru.T], axis=1), jnp.concatenate([ru, rr], axis=1)], axis=0)
+        tw = dot(g, w)
+        w_ref[t] = w
+        t_ref[t] = tw
+        gram_ref[t] = dot(w, tw, 0, 0)
 
     others(lambda b: vg.copy(rv_hbm.at[0], vblk.at[at.c], b).wait_send(), later)
-    others(lambda b: rg.copy(ru_hbm.at[0], rblock(at.c), b).wait_send())
     others(lambda b: pg.copy(zsend.at[b], zpart.at[at.c], b).wait_send(), earlier)
-    others(lambda b: qg.copy(zt.at[at.c], zt.at[at.c], b).wait_send())
+    rg.drain()
+    qg.drain()
     cv.drain()
     cu.drain()
     out_r.wait()
     out_c.wait()
 
 
-def spread_panels(row_v, row_u, col_u, col_v, diag, tiles):
+def spread_panels(row_v, row_u, col_u, col_v, diag, tile_u, tile_v, sketch):
     cols = lax.axis_size("col")
+    tiles = tile_u.shape[0]
     part, k = row_v.shape[1:]
     rows = cols * part
     vm = pl.BlockSpec(memory_space=pltpu.VMEM)
-    hbm = pl.BlockSpec(memory_space=pl.ANY)
+    hbm = pl.BlockSpec(memory_space=pltpu.HBM)
     dma = pltpu.SemaphoreType.DMA
     return pl.pallas_call(
         panel_kernel,
         name="spread_panels",
         out_shape=(
+            jax.ShapeDtypeStruct((tiles, 2 * k, k), f32),
+            jax.ShapeDtypeStruct((tiles, 2 * k, k), f32),
+            jax.ShapeDtypeStruct((tiles, k, k), f32),
             jax.ShapeDtypeStruct((tiles, k, k), f32),
             jax.ShapeDtypeStruct((rows, k), f32),
             jax.ShapeDtypeStruct((tiles, rows, k), f32),
         ),
-        in_specs=[hbm] * 5,
-        out_specs=(vm, hbm, hbm),
+        in_specs=[hbm] * 7 + [vm],
+        out_specs=(vm, vm, vm, vm, hbm, hbm),
         scratch_shapes=[
             pltpu.VMEM((cols, part, k), f32),
+            pltpu.VMEM((rows, 2 * k), bf16),
             pltpu.VMEM((rows, k), f32),
+            pltpu.VMEM((rows, 2 * k), bf16),
             pltpu.VMEM((part, rows), f32),
-            pltpu.VMEM((cols, part, 2 * part), bf16),
-            pltpu.VMEM((part, 2 * k), f32),
+            pltpu.VMEM((2, part, rows), bf16),
             pltpu.VMEM((cols, k, part), f32),
             pltpu.VMEM((cols, k, part), f32),
             pltpu.VMEM((cols, k, part), f32),
@@ -527,20 +651,31 @@
             pltpu.VMEM((tiles, rows, k), f32),
             pltpu.VMEM((tiles, rows, k), f32),
             pltpu.VMEM((rows, 2 * k), bf16),
+            pltpu.VMEM((tiles, rows, k), f32),
+            pltpu.VMEM((tiles, rows, k), f32),
+            pltpu.VMEM((tiles, rows, 2 * k), bf16),
+            pltpu.VMEM((2 * k, rows), bf16),
+            pltpu.VMEM((2 * k, rows), bf16),
+            pltpu.VMEM((tiles, k, k), f32),
+            pltpu.VMEM((tiles, k, k), f32),
+            pltpu.VMEM((tiles, k, k), f32),
         ]
-        + [dma((cols,))] * 8
+        + [dma((cols,))] * 4
+        + ([dma((1,))] * 2 + [dma((2, 2))] * 4) * 2
         + [dma((2,))] * 4
         + [dma((2, 2, 2))] * 4
         + [dma((2, 10))] * 2
-        + [dma((2,)), dma((3,)), dma((2,))],
-        compiler_params=pltpu.CompilerParams(collective_id=0, has_side_effects=True, vmem_limit_bytes=50 * 2**20),
+        + [dma((2,)), dma((3,)), dma((2,)), dma((2, tiles))],
+        compiler_params=pltpu.CompilerParams(collective_id=0, has_side_effects=True, vmem_limit_bytes=54 * 2**20),
         cost_estimate=pl.CostEstimate(flops=10**9, bytes_accessed=16 * 2**20, transcendentals=0),
-    )(row_v, row_u, col_u, col_v, diag)
+    )(row_v, row_u, col_u, col_v, diag, tile_u, tile_v, sketch)
 
 
 def body(tile_u, tile_v, row_panel_u, row_panel_v, col_panel_u, col_panel_v, diag_inverse, sketch):
-    cores, row_u, col_u = spread_panels(row_panel_v, row_panel_u, col_panel_u, col_panel_v, diag_inverse, tile_u.shape[1])
-    new_u, new_v = recompress(tile_u[0], tile_v[0], row_u, col_u, cores, sketch)
+    w, tw, gram, cores, row_u, col_u = spread_panels(
+        row_panel_v, row_panel_u, col_panel_u, col_panel_v, diag_inverse, tile_u[0], tile_v[0], sketch
+    )
+    new_u, new_v = recompress(tile_u[0], tile_v[0], row_u, col_u, cores, w, tw, gram)
     return new_u[None], new_v[None]
 
 

time: 142 us -> 109 us (0.77)
  the two profiles are of different devices: /device:TPU:1 before, /device:TPU:6 now
where the time goes in v2:
time: 109 us
  Pallas kernels  108 us (99%)
    pallas_call x1, Pallas kernels, spread_panels(): pl.pallas_call(panel_kernel, name='spread_panels', out_shape=(jax.ShapeDt...  80.9 us
    pallas_call x1, Pallas kernels, recompress(): pl.pallas_call(finish_kernel, name='recompress', out_shape=(out, out), in...  26.8 us

profile of v2, /device:TPU:6, one launch (start us, length us, event | category | flops | bytes accessed | tf_op | source)
XLA Modules:
  0.0 108.5 jit_solution(1263530043969049815)
XLA Ops:
  0.6 80.9 %spread_panels.1 = (f32[4,256,128]{2,1,0:T(8,128)}, f32[4,256,128]{2,1,0:T(8,128)}, f32[4,128,128]{2,1,0:T(8,128)}, f32[4,128,128]{2,1,0:T(8,128)}, f32[2048,128]{1,0:T(8,128)}, /*index=5*/f32[4,2048,128]{2,1,0:T(8,128)}) custom-call(f32[1,256,128]{2,1,0:T(8,128)} %rv_hbm.1, f32[1,256,128]{2,1,0:T(8,128)} %ru_hbm.1, f32[2,256,128]{2,1,0:T(8,128)} %cu_hbm.1, ...), custom_call_target="tpu_custom_call" | custom-call | flops 1000000000 | bytes 16777216 | tf_op jit(solution)/shard_map/spread_panels/pallas_call | solution.py:627
  81.6 26.8 %recompress.1 = (f32[4,2048,128]{2,1,0:T(8,128)}, f32[4,2048,128]{2,1,0:T(8,128)}) custom-call(f32[4,2048,128]{2,1,0:T(8,128)} %bitcast.5, f32[4,2048,128]{2,1,0:T(8,128)} %bitcast.7, f32[2048,128]{1,0:T(8,128)} %get-tuple-element.10.r_hbm, f32[4,2048,128]{2,1,0:T(8,128)} %get-tuple-element.11.c_hbm, f32[4,128,128]{2,1,0:T(8,128)} %get-tuple-element.12.cores_hbm, ...), custom_call_target="tpu_custom_call" | custom-call | flops 10000000000 | bytes 25165824 | tf_op jit(solution)/shard_map/recompress/pallas_call | solution.py:135

commit v3 on v2

--- a/solution.py
+++ b/solution.py
@@ -9,6 +9,7 @@
 
 highest = lax.Precision.HIGHEST
 f32, bf16 = jnp.float32, jnp.bfloat16
+STEP = 2048
 
 
 def halves(x):
@@ -34,6 +35,21 @@
 
 def dotb(a, b, ca=1, cb=0):
     return lax.dot_general(a, b, (((ca,), (cb,)), ((), ())), preferred_element_type=f32)
+
+
+def split3(x):
+    hi = x.astype(bf16).astype(f32)
+    rest = x - hi
+    mid = rest.astype(bf16).astype(f32)
+    return hi, mid, rest - mid
+
+
+def outer(a, b):
+    ah, am, al = split3(a)
+    bh, bm, bl = split3(b)
+    left = jnp.concatenate([ah, am, ah, al, ah, am], axis=0).astype(bf16)
+    right = jnp.concatenate([bh, bh, bm, bh, bl, bm], axis=0).astype(bf16)
+    return dotb(left, right, 0, 0)
 
 
 def inverse_factors(gram_ref, inv_ref, fac_ref):
@@ -66,7 +82,7 @@
             lower = panel * scale
             for t in range(tiles):
                 both = jnp.concatenate([panel[t], own[t]], axis=1)
-                upd = dot(lower[t], both, 0, 0)
+                upd = outer(lower[t], both)
                 gram_ref[t, lo + 8 :, :] = gram_ref[t, lo + 8 :, :] - upd[lo + 8 :, :k]
                 if p == 0:
                     inv_ref[t, lo + 8 :, :] = -upd[lo + 8 :, k:]
@@ -75,9 +91,9 @@
 
 
 def finish_kernel(u_hbm, v_hbm, r_hbm, c_hbm, cores_hbm, w_hbm, t_hbm, gram_hbm, nu_hbm, nv_hbm,
-                  ubuf, vbuf, cbuf, rbuf, cores_ref, w_ref, t_ref, gram_s, inv_s, fac_s, in_sem, r_sem, out_sem):
-    tiles, rows, k = ubuf.shape
-    step = min(512, rows)
+                  ubuf, vbuf, cbuf, rbuf, uout, vout, cores_ref, w_ref, t_ref, gram_s, inv_s, fac_s, wide_s, in_sem, r_sem, out_sem):
+    tiles, rows, k = uout.shape
+    step = min(STEP, rows)
     scaling = math.sqrt(rows)
 
     def load(t, which):
@@ -97,27 +113,28 @@
     inverse_factors(gram_s, inv_s, fac_s)
 
     def store(t, which):
-        src, dst = ((ubuf, nu_hbm), (vbuf, nv_hbm))[which]
+        src, dst = ((uout, nu_hbm), (vout, nv_hbm))[which]
         return pltpu.make_async_copy(src.at[t], dst.at[t], out_sem.at[which, t])
 
     for copy in singles[1:]:
         copy.wait()
     for t in range(tiles):
-        for which in range(3):
-            load(t, which).wait()
         fac = fac_s[t]
         x = dot(w_ref[t], fac, 1, 1) * scaling
         y = dot(t_ref[t], fac, 1, 1) * (1.0 / scaling)
-        c1 = y[:k]
         c2 = -dot(cores_ref[t], y[k:], 0, 0)
-        x1, x2, c1, c2 = doubled(x[:k]), doubled(x[k:]), doubled(c1), doubled(c2)
-
-        def finish(n, carry, t=t, x1=x1, x2=x2, c1=c1, c2=c2):
+        for n, part in enumerate((x[:k], x[k:], y[:k], c2)):
+            wide_s[t, n] = doubled(part)
+    for t in range(tiles):
+        for which in range(3):
+            load(t, which).wait()
+
+        def finish(n, carry, t=t):
             at = pl.ds(pl.multiple_of(n * step, step), step)
-            a = dotb(halves(ubuf[t, at, :]), x1) + dotb(halves(rbuf[at, :]), x2)
-            ubuf[t, at, :] = a[:, :k] + a[:, k:]
-            b = dotb(halves(vbuf[t, at, :]), c1) + dotb(halves(cbuf[t, at, :]), c2)
-            vbuf[t, at, :] = b[:, :k] + b[:, k:]
+            a = dotb(ubuf[t, at, :], wide_s[t, 0]) + dotb(rbuf[at, :], wide_s[t, 1])
+            uout[t, at, :] = a[:, :k] + a[:, k:]
+            b = dotb(vbuf[t, at, :], wide_s[t, 2]) + dotb(cbuf[t, at, :], wide_s[t, 3])
+            vout[t, at, :] = b[:, :k] + b[:, k:]
             return carry
 
         lax.fori_loop(0, rows // step, finish, 0)
@@ -129,9 +146,9 @@
 
 
 def recompress(tile_u, tile_v, row_u, col_u, cores, w, tw, gram):
-    tiles, rows, k = tile_u.shape
+    tiles, rows, k = tile_u.shape[0], tile_u.shape[1], cores.shape[1]
     hbm = pl.BlockSpec(memory_space=pltpu.HBM)
-    out = jax.ShapeDtypeStruct(tile_u.shape, f32)
+    out = jax.ShapeDtypeStruct((tiles, rows, k), f32)
     return pl.pallas_call(
         finish_kernel,
         name="recompress",
@@ -139,16 +156,19 @@
         in_specs=[hbm] * 8,
         out_specs=(hbm, hbm),
         scratch_shapes=[
+            pltpu.VMEM((tiles, rows, 2 * k), bf16),
+            pltpu.VMEM((tiles, rows, 2 * k), bf16),
+            pltpu.VMEM((tiles, rows, 2 * k), bf16),
+            pltpu.VMEM((rows, 2 * k), bf16),
             pltpu.VMEM((tiles, rows, k), f32),
             pltpu.VMEM((tiles, rows, k), f32),
-            pltpu.VMEM((tiles, rows, k), f32),
-            pltpu.VMEM((rows, k), f32),
             pltpu.VMEM((tiles, k, k), f32),
             pltpu.VMEM((tiles, 2 * k, k), f32),
             pltpu.VMEM((tiles, 2 * k, k), f32),
             pltpu.VMEM((tiles, k, k), f32),
             pltpu.VMEM((tiles, k, k), f32),
             pltpu.VMEM((tiles, k, k), f32),
+            pltpu.VMEM((tiles, 4, 2 * k, 2 * k), bf16),
             pltpu.SemaphoreType.DMA((3, tiles)),
             pltpu.SemaphoreType.DMA((5,)),
             pltpu.SemaphoreType.DMA((2, tiles)),
@@ -320,7 +340,7 @@
             self.d_copy(n).wait_send()
 
 
-def greet(at):
+def greet(at, before_wait):
     barrier = pltpu.get_barrier_semaphore()
 
     def hello(device):
@@ -337,6 +357,11 @@
     def _():
         hello(at.target)
         hello(at.source)
+
+    before_wait()
+
+    @pl.when(jnp.logical_not(at.alone))
+    def _():
         pl.semaphore_wait(barrier, at.cols + 5)
 
     @pl.when(at.alone)
@@ -414,11 +439,11 @@
                 self.f_copy(s, to).wait_send()
 
 
-def panel_kernel(rv_hbm, ru_hbm, cu_hbm, cv_hbm, d_hbm, u_hbm, v_hbm, s_ref, w_ref, t_ref, gram_ref, cores_ref, r_hbm, c_hbm,
-                 vblk, vsp, rbuf, rsp, dbuf, dsp, zpart, zsend, zt, zsp, cub, cvb, csp, ubuf, vbuf, usp, tts, ttr, uu_s, p1_s, ru_s,
+def panel_kernel(rv_hbm, ru_hbm, cu_hbm, cv_hbm, d_hbm, u_hbm, v_hbm, s_ref, w_ref, t_ref, gram_ref, cores_ref, rs_hbm, us_hbm, vs_hbm, cs_hbm,
+                 vblk, vsp, rbuf, rsp, dbuf, dsp, zpart, zsend, zt, zsp, cub, cvb, csp, xsp, ubuf, vbuf, usp, wsp, tts, ttr, uu_s, p1_s, p2_s, ru_s,
                  v_send, v_recv, p_send, p_recv, rz_send, rz_recv, ry_send, ry_recv, rf_send, rf_recv,
                  qz_send, qz_recv, qy_send, qy_recv, qf_send, qf_recv,
-                 t_send, t_recv, z_send, z_recv, x_send, x_recv, f_send, f_recv, d_send, d_recv, own_sem, in_sem, out_sem, uv_sem):
+                 t_send, t_recv, z_send, z_recv, x_send, x_recv, f_send, f_recv, d_send, d_recv, own_sem, in_sem, out_sem, uv_sem, save_sem):
     cols, part, k = vblk.shape
     tiles = ubuf.shape[0]
     rows = cols * part
@@ -466,24 +491,13 @@
         src, dst = ((u_hbm, ubuf), (v_hbm, vbuf))[which]
         return pltpu.make_async_copy(src.at[t], dst.at[t], uv_sem.at[which, t])
 
+    def save(n, t):
+        src, dst = ((usp, us_hbm), (wsp, vs_hbm), (csp, cs_hbm))[n]
+        return pltpu.make_async_copy(src.at[t], dst.at[t], save_sem.at[n, t])
+
     load_d.start()
     load_v.start()
     load_r.start()
-    greet(at)
-    others(lambda b: vg.copy(rv_hbm.at[0], vblk.at[at.c], b).start(), later)
-    cv.transpose_start()
-    cu.transpose_start()
-    for t in range(tiles):
-        load_tile(t, 0).start()
-        load_tile(t, 1).start()
-
-    for b in range(cols):
-
-        @pl.when(b > at.c)
-        def _(b=b):
-            vsp[part * b : part * (b + 1), :] = jnp.zeros((part, 2 * k), bf16)
-
-    load_d.wait()
 
     def split_d(b, carry):
         d = dbuf[:, span(b)]
@@ -492,7 +506,25 @@
         dsp[1, :, span(b)] = (d - hi.astype(f32)).astype(bf16)
         return carry
 
-    lax.fori_loop(0, cols, split_d, 0)
+    def prepare():
+        for b in range(cols):
+
+            @pl.when(b > at.c)
+            def _(b=b):
+                vsp[part * b : part * (b + 1), :] = jnp.zeros((part, 2 * k), bf16)
+
+        load_v.wait()
+        vsp[span(at.c), :] = halves(vblk[at.c])
+        load_d.wait()
+        lax.fori_loop(0, cols, split_d, 0)
+
+    greet(at, prepare)
+    others(lambda b: vg.copy(rv_hbm.at[0], vblk.at[at.c], b).start(), later)
+    cv.transpose_start()
+    cu.transpose_start()
+    for t in range(tiles):
+        load_tile(t, 0).start()
+        load_tile(t, 1).start()
 
     def split_s(b, carry):
         tts[:, span(b)] = halves(s_ref[span(b), :]).astype(f32).T.astype(bf16)
@@ -507,18 +539,26 @@
 
         lax.fori_loop(0, cols, body, 0)
 
+    def split_all(dst, src):
+        def body(b, carry):
+            for t in range(tiles):
+                dst[t, span(b), :] = halves(src[t, span(b), :])
+            return carry
+
+        lax.fori_loop(0, cols, body, 0)
+
     def tile_products(t):
         load_tile(t, 0).wait()
         load_tile(t, 1).wait()
         split_into(usp.at[t], ubuf.at[t])
+        split_into(wsp.at[t], vbuf.at[t])
+        save(0, t).start()
+        save(1, t).start()
         uu_s[t] = fold4(dotb(usp[t], usp[t], 0, 0))
-        split_into(csp, vbuf.at[t])
-        p1_s[t] = fold4(dotb(tts[...], csp[...]))
+        p1_s[t] = fold4(dotb(tts[...], wsp[t]))
 
     cv.stage_own()
     cu.stage_own()
-    load_v.wait()
-    vsp[span(at.c), :] = halves(vblk[at.c])
 
     def arrived(b, carry):
         vg.wait_from(vblk.at[b], b)
@@ -538,7 +578,6 @@
     rg.stage_own()
     tile_products(0)
     cv.stage_forward(0)
-    cu.stage_forward(0)
     zt[at.c] = zsend[at.c]
 
     def gather(n, carry):
@@ -549,25 +588,22 @@
 
     lax.fori_loop(0, cols - 1 - at.c, gather, 0)
     qg.stage_own()
+    cv.stage_forward(1)
     rg.stage_partner()
     tile_products(1)
     qg.stage_partner()
-    cv.stage_forward(1)
-    cu.stage_forward(1)
+    cu.stage_forward(0)
     rg.stage_forward(0)
     qg.stage_forward(0)
+    cv.stage_far(0)
+    cv.stage_far(1)
     tile_products(2)
     rg.stage_forward(1)
     qg.stage_forward(1)
+    cu.stage_forward(1)
     tile_products(3)
-    cv.stage_far(0)
-    cu.stage_far(0)
-    cv.stage_far(1)
-    cu.stage_far(1)
     rg.stage_far(0)
     rg.stage_far(1)
-    out_r = pltpu.make_async_copy(rbuf, r_hbm, out_sem.at[0])
-    out_r.start()
 
     def split_r(b, carry):
         h = halves(rbuf[span(b), :])
@@ -576,9 +612,15 @@
         return carry
 
     lax.fori_loop(0, cols, split_r, 0)
+    out_r = pltpu.make_async_copy(rsp, rs_hbm, out_sem.at[0])
+    out_r.start()
     rr = fold4(dotb(ttr[...], rsp[...]))
     for t in range(tiles):
         ru_s[t] = fold4(dotb(ttr[...], usp[t]))
+    cv.stage_other_core()
+    cu.stage_far(0)
+    cu.stage_far(1)
+    split_all(xsp, cvb)
     qg.stage_far(0)
     qg.stage_far(1)
     for b in range(cols):
@@ -586,25 +628,27 @@
         hi = z.astype(bf16)
         zsp[:k, part * b : part * (b + 1)] = hi
         zsp[k:, part * b : part * (b + 1)] = (z - hi.astype(f32)).astype(bf16)
-    cv.stage_other_core()
-    for t in range(tiles):
-        split_into(csp, cvb.at[t])
-        cores_ref[t] = fold4(dotb(zsp[...], csp[...]))
+    for t in range(tiles):
+        cores_ref[t] = fold4(dotb(zsp[...], xsp[t]))
     cu.stage_other_core()
-    out_c = pltpu.make_async_copy(cub, c_hbm, out_sem.at[1])
-    out_c.start()
-    for t in range(tiles):
-        split_into(csp, cub.at[t])
-        p2t = fold4(dotb(tts[...], csp[...]))
-        w1 = p1_s[t].T
-        w2 = -dot(cores_ref[t], p2t, 1, 1)
-        w = jnp.concatenate([w1, w2], axis=0)
+    split_all(csp, cub)
+    for t in range(tiles):
+        save(2, t).start()
+    for t in range(tiles):
+        p2_s[t] = fold4(dotb(tts[...], csp[t]))
+    ws = []
+    for t in range(tiles):
+        w2 = -dot(cores_ref[t], p2_s[t], 1, 1)
+        ws.append(jnp.concatenate([p1_s[t].T, w2], axis=0))
+        w_ref[t] = ws[t]
+    tws = []
+    for t in range(tiles):
         ru = ru_s[t]
         g = jnp.concatenate([jnp.concatenate([uu_s[t], ru.T], axis=1), jnp.concatenate([ru, rr], axis=1)], axis=0)
-        tw = dot(g, w)
-        w_ref[t] = w
-        t_ref[t] = tw
-        gram_ref[t] = dot(w, tw, 0, 0)
+        tws.append(dot(g, ws[t]))
+        t_ref[t] = tws[t]
+    for t in range(tiles):
+        gram_ref[t] = dot(ws[t], tws[t], 0, 0)
 
     others(lambda b: vg.copy(rv_hbm.at[0], vblk.at[at.c], b).wait_send(), later)
     others(lambda b: pg.copy(zsend.at[b], zpart.at[at.c], b).wait_send(), earlier)
@@ -613,7 +657,9 @@
     cv.drain()
     cu.drain()
     out_r.wait()
-    out_c.wait()
+    for t in range(tiles):
+        for n in range(3):
+            save(n, t).wait()
 
 
 def spread_panels(row_v, row_u, col_u, col_v, diag, tile_u, tile_v, sketch):
@@ -632,11 +678,13 @@
             jax.ShapeDtypeStruct((tiles, 2 * k, k), f32),
             jax.ShapeDtypeStruct((tiles, k, k), f32),
             jax.ShapeDtypeStruct((tiles, k, k), f32),
-            jax.ShapeDtypeStruct((rows, k), f32),
-            jax.ShapeDtypeStruct((tiles, rows, k), f32),
+            jax.ShapeDtypeStruct((rows, 2 * k), bf16),
+            jax.ShapeDtypeStruct((tiles, rows, 2 * k), bf16),
+            jax.ShapeDtypeStruct((tiles, rows, 2 * k), bf16),
+            jax.ShapeDtypeStruct((tiles, rows, 2 * k), bf16),
         ),
         in_specs=[hbm] * 7 + [vm],
-        out_specs=(vm, vm, vm, vm, hbm, hbm),
+        out_specs=(vm, vm, vm, vm, hbm, hbm, hbm, hbm),
         scratch_shapes=[
             pltpu.VMEM((cols, part, k), f32),
             pltpu.VMEM((rows, 2 * k), bf16),
@@ -650,12 +698,15 @@
             pltpu.VMEM((2 * k, rows), bf16),
             pltpu.VMEM((tiles, rows, k), f32),
             pltpu.VMEM((tiles, rows, k), f32),
-            pltpu.VMEM((rows, 2 * k), bf16),
+            pltpu.VMEM((tiles, rows, 2 * k), bf16),
+            pltpu.VMEM((tiles, rows, 2 * k), bf16),
             pltpu.VMEM((tiles, rows, k), f32),
             pltpu.VMEM((tiles, rows, k), f32),
             pltpu.VMEM((tiles, rows, 2 * k), bf16),
+            pltpu.VMEM((tiles, rows, 2 * k), bf16),
             pltpu.VMEM((2 * k, rows), bf16),
             pltpu.VMEM((2 * k, rows), bf16),
+            pltpu.VMEM((tiles, k, k), f32),
             pltpu.VMEM((tiles, k, k), f32),
             pltpu.VMEM((tiles, k, k), f32),
             pltpu.VMEM((tiles, k, k), f32),
@@ -665,17 +716,17 @@
         + [dma((2,))] * 4
         + [dma((2, 2, 2))] * 4
         + [dma((2, 10))] * 2
-        + [dma((2,)), dma((3,)), dma((2,)), dma((2, tiles))],
+        + [dma((2,)), dma((3,)), dma((1,)), dma((2, tiles)), dma((3, tiles))],
         compiler_params=pltpu.CompilerParams(collective_id=0, has_side_effects=True, vmem_limit_bytes=54 * 2**20),
         cost_estimate=pl.CostEstimate(flops=10**9, bytes_accessed=16 * 2**20, transcendentals=0),
     )(row_v, row_u, col_u, col_v, diag, tile_u, tile_v, sketch)
 
 
 def body(tile_u, tile_v, row_panel_u, row_panel_v, col_panel_u, col_panel_v, diag_inverse, sketch):
-    w, tw, gram, cores, row_u, col_u = spread_panels(
+    w, tw, gram, cores, row_u, split_u, split_v, col_u = spread_panels(
         row_panel_v, row_panel_u, col_panel_u, col_panel_v, diag_inverse, tile_u[0], tile_v[0], sketch
     )
-    new_u, new_v = recompress(tile_u[0], tile_v[0], row_u, col_u, cores, w, tw, gram)
+    new_u, new_v = recompress(split_u, split_v, row_u, col_u, cores, w, tw, gram)
     return new_u[None], new_v[None]
 
 

time: 109 us -> 97 us (0.89)
  the two profiles are of different devices: /device:TPU:6 before, /device:TPU:1 now
where the time goes in v3:
time: 97 us; the launch traced here: 96.8 us
  Pallas kernels  96 us (99%)
    pallas_call x1, Pallas kernels, spread_panels(): pl.pallas_call(panel_kernel, name='spread_panels', out_shape=(jax.ShapeDt...  77.2 us
    pallas_call x1, Pallas kernels, recompress(): pl.pallas_call(finish_kernel, name='recompress', out_shape=(out, out), in...  18.8 us

profile of v3, /device:TPU:1, one launch (start us, length us, event | category | flops | bytes accessed | tf_op | source)
XLA Modules:
  0.0 96.8 jit_solution(12608497934005737510)
XLA Ops:
  0.6 77.2 %spread_panels.1 = (f32[4,256,128]{2,1,0:T(8,128)}, f32[4,256,128]{2,1,0:T(8,128)}, f32[4,128,128]{2,1,0:T(8,128)}, f32[4,128,128]{2,1,0:T(8,128)}, bf16[2048,25...) custom-call(f32[1,256,128]{2,1,0:T(8,128)} %rv_hbm.1, ...), custom_call_target="tpu_custom_call" | custom-call | flops 1000000000 | bytes 16777216 | tf_op jit(solution)/shard_map/spread_panels/pallas_call | solution.py:673
  77.8 18.8 %recompress.1 = (f32[4,2048,128]{2,1,0:T(8,128)}, f32[4,2048,128]{2,1,0:T(8,128)}) custom-call(bf16[4,2048,256]{2,1,0:T(8,128)(2,1)} %get-tuple-element.12.u_hbm, bf16[4,2048,256]{2,1,0:T(8,128)(2,1)} %get-tuple-element.13.v_hbm, bf16[2048,256]{1,0:T(8,128)(2,1)} %get-tuple-element.14.r_hbm, bf16[4,2048,256]{2,1,0:T(8,128)(2,1)} %get-tuple-element.15.c_hbm, ...), custom_call_target="tpu_custom_call" | custom-call | flops 10000000000 | bytes 25165824 | tf_op jit(solution)/shard_map/recompress/pallas_call | solution.py:152

commit v4 on v3

--- a/solution.py
+++ b/solution.py
@@ -198,10 +198,11 @@
         self.m = lax.div(self.r, 2)
         self.x = lax.rem(self.m, 4)
         self.zl = lax.div(self.m, 4)
-        self.mixed = mix(self.m, self.c)
+        self.turn = 6 * self.core
+        self.mixed = mix(mix(self.m, self.c), self.turn)
         self.target = (2 * self.mixed + self.core, self.m)
         self.source = (2 * self.c + self.core, self.mixed)
-        self.alone = jnp.logical_and(self.m == 0, self.c == 0)
+        self.alone = jnp.logical_and(self.m == self.c, self.c == self.turn)
 
     def chip(self, zl, x):
         return 4 * zl + x
@@ -230,7 +231,7 @@
 
     def block(self, m, core=None, tile=None):
         core = self.at.core if core is None else core
-        rows = pl.ds(pl.multiple_of(mix(m, self.at.c) * self.rows, self.rows), self.rows)
+        rows = pl.ds(pl.multiple_of(mix(mix(m, self.at.c), 6 * core) * self.rows, self.rows), self.rows)
         if tile is None:
             return self.buf.at[pl.ds(2 * core, 2), rows, :]
         return self.buf.at[pl.ds(2 * core + tile, 1), rows, :]
@@ -547,6 +548,18 @@
 
         lax.fori_loop(0, cols, body, 0)
 
+    def use_pair(core):
+        def body(b, carry):
+            for i in range(2):
+                csp[2 * core + i, span(b), :] = halves(cub[2 * core + i, span(b), :])
+            return carry
+
+        lax.fori_loop(0, cols, body, 0)
+        for i in range(2):
+            save(2, 2 * core + i).start()
+        for i in range(2):
+            p2_s[2 * core + i] = fold4(dotb(tts[...], csp[2 * core + i]))
+
     def tile_products(t):
         load_tile(t, 0).wait()
         load_tile(t, 1).wait()
@@ -577,7 +590,6 @@
     load_r.wait()
     rg.stage_own()
     tile_products(0)
-    cv.stage_forward(0)
     zt[at.c] = zsend[at.c]
 
     def gather(n, carry):
@@ -588,23 +600,23 @@
 
     lax.fori_loop(0, cols - 1 - at.c, gather, 0)
     qg.stage_own()
+    cv.stage_forward(0)
     cv.stage_forward(1)
     rg.stage_partner()
     tile_products(1)
     qg.stage_partner()
+    qg.stage_forward(0)
     cu.stage_forward(0)
     rg.stage_forward(0)
-    qg.stage_forward(0)
+    tile_products(2)
+    qg.stage_forward(1)
+    rg.stage_forward(1)
     cv.stage_far(0)
     cv.stage_far(1)
-    tile_products(2)
-    rg.stage_forward(1)
-    qg.stage_forward(1)
     cu.stage_forward(1)
     tile_products(3)
     rg.stage_far(0)
     rg.stage_far(1)
-
     def split_r(b, carry):
         h = halves(rbuf[span(b), :])
         rsp[span(b), :] = h
@@ -630,12 +642,9 @@
         zsp[k:, part * b : part * (b + 1)] = (z - hi.astype(f32)).astype(bf16)
     for t in range(tiles):
         cores_ref[t] = fold4(dotb(zsp[...], xsp[t]))
+    use_pair(at.core)
     cu.stage_other_core()
-    split_all(csp, cub)
-    for t in range(tiles):
-        save(2, t).start()
-    for t in range(tiles):
-        p2_s[t] = fold4(dotb(tts[...], csp[t]))
+    use_pair(1 - at.core)
     ws = []
     for t in range(tiles):
         w2 = -dot(cores_ref[t], p2_s[t], 1, 1)

time: 97 us -> 95.8 us (0.988); the launches traced: 96.8 us -> 94 us
  Pallas kernels: 96 us -> 93.2 us
    pallas_call x1, Pallas kernels: 77.2 us -> 74.3 us  [spread_panels(): pl.pallas_call(panel_kernel, name='spread_panels', out_shape=(jax.ShapeDt...]
where the time goes in v4:
time: 95.8 us; the launch traced here: 94 us
  Pallas kernels  93.2 us (97%)
    pallas_call x1, Pallas kernels, spread_panels(): pl.pallas_call(panel_kernel, name='spread_panels', out_shape=(jax.ShapeDt...  74.3 us
    pallas_call x1, Pallas kernels, recompress(): pl.pallas_call(finish_kernel, name='recompress', out_shape=(out, out), in...  18.8 us

profile of v4, /device:TPU:1, one launch (start us, length us, event | category | flops | bytes accessed | tf_op | source)
XLA Modules:
  0.0 94.0 jit_solution(6780786127274807679)
XLA Ops:
  0.6 74.3 %spread_panels.1 = (f32[4,256,128]{2,1,0:T(8,128)}, f32[4,256,128]{2,1,0:T(8,128)}, f32[4,128,128]{2,1,0:T(8,128)}, f32[4,128,128]{2,1,0:T(8,128)}, bf16[2048,25...) custom-call(f32[1,256,128]{2,1,0:T(8,128)} %rv_hbm.1, ...), custom_call_target="tpu_custom_call" | custom-call | flops 1000000000 | bytes 16777216 | tf_op jit(solution)/shard_map/spread_panels/pallas_call | solution.py:682
  75.0 18.8 %recompress.1 = (f32[4,2048,128]{2,1,0:T(8,128)}, f32[4,2048,128]{2,1,0:T(8,128)}) custom-call(bf16[4,2048,256]{2,1,0:T(8,128)(2,1)} %get-tuple-element.12.u_hbm, bf16[4,2048,256]{2,1,0:T(8,128)(2,1)} %get-tuple-element.13.v_hbm, bf16[2048,256]{1,0:T(8,128)(2,1)} %get-tuple-element.14.r_hbm, bf16[4,2048,256]{2,1,0:T(8,128)(2,1)} %get-tuple-element.15.c_hbm, ...), custom_call_target="tpu_custom_call" | custom-call | flops 10000000000 | bytes 25165824 | tf_op jit(solution)/shard_map/recompress/pallas_call | solution.py:152

commit v5 on v4

--- a/solution.py
+++ b/solution.py
@@ -35,6 +35,12 @@
 
 def dotb(a, b, ca=1, cb=0):
     return lax.dot_general(a, b, (((ca,), (cb,)), ((), ())), preferred_element_type=f32)
+
+
+def dot4(a, b):
+    n = b.shape[1]
+    q = dotb(halves(a), doubled(b))
+    return q[:, :n] + q[:, n:]
 
 
 def split3(x):
@@ -120,9 +126,10 @@
         copy.wait()
     for t in range(tiles):
         fac = fac_s[t]
-        x = dot(w_ref[t], fac, 1, 1) * scaling
-        y = dot(t_ref[t], fac, 1, 1) * (1.0 / scaling)
-        c2 = -dot(cores_ref[t], y[k:], 0, 0)
+        fac_t = fac.T
+        x = dot4(w_ref[t], fac_t) * scaling
+        y = dot4(t_ref[t], fac_t) * (1.0 / scaling)
+        c2 = -dot4(cores_ref[t].T, y[k:])
         for n, part in enumerate((x[:k], x[k:], y[:k], c2)):
             wide_s[t, n] = doubled(part)
     for t in range(tiles):
@@ -647,17 +654,17 @@
     use_pair(1 - at.core)
     ws = []
     for t in range(tiles):
-        w2 = -dot(cores_ref[t], p2_s[t], 1, 1)
+        w2 = -dot4(cores_ref[t], p2_s[t].T)
         ws.append(jnp.concatenate([p1_s[t].T, w2], axis=0))
         w_ref[t] = ws[t]
     tws = []
     for t in range(tiles):
         ru = ru_s[t]
         g = jnp.concatenate([jnp.concatenate([uu_s[t], ru.T], axis=1), jnp.concatenate([ru, rr], axis=1)], axis=0)
-        tws.append(dot(g, ws[t]))
+        tws.append(dot4(g, ws[t]))
         t_ref[t] = tws[t]
     for t in range(tiles):
-        gram_ref[t] = dot(ws[t], tws[t], 0, 0)
+        gram_ref[t] = dot4(ws[t].T, tws[t])
 
     others(lambda b: vg.copy(rv_hbm.at[0], vblk.at[at.c], b).wait_send(), later)
     others(lambda b: pg.copy(zsend.at[b], zpart.at[at.c], b).wait_send(), earlier)

time: 95.8 us -> 93.8 us (0.979)
  Pallas kernels: 93.2 us -> 91.2 us
    pallas_call x1, Pallas kernels: 74.3 us -> 73.2 us  [spread_panels(): pl.pallas_call(panel_kernel, name='spread_panels', out_shape=(jax.ShapeDt...]
where the time goes in v5:
time: 93.8 us; the launch traced here: 92 us
  Pallas kernels  91.2 us (97%)
    pallas_call x1, Pallas kernels, spread_panels(): pl.pallas_call(panel_kernel, name='spread_panels', out_shape=(jax.ShapeDt...  73.2 us
    pallas_call x1, Pallas kernels, recompress(): pl.pallas_call(finish_kernel, name='recompress', out_shape=(out, out), in...  18.1 us

profile of v5, /device:TPU:1, one launch (start us, length us, event | category | flops | bytes accessed | tf_op | source)
XLA Modules:
  0.0 92.0 jit_solution(11165977458726788766)
XLA Ops:
  0.6 73.2 %spread_panels.1 = (f32[4,256,128]{2,1,0:T(8,128)}, f32[4,256,128]{2,1,0:T(8,128)}, f32[4,128,128]{2,1,0:T(8,128)}, f32[4,128,128]{2,1,0:T(8,128)}, bf16[2048,25...) custom-call(f32[1,256,128]{2,1,0:T(8,128)} %rv_hbm.1, ...), custom_call_target="tpu_custom_call" | custom-call | flops 1000000000 | bytes 16777216 | tf_op jit(solution)/shard_map/spread_panels/pallas_call | solution.py:689
  73.8 18.1 %recompress.1 = (f32[4,2048,128]{2,1,0:T(8,128)}, f32[4,2048,128]{2,1,0:T(8,128)}) custom-call(bf16[4,2048,256]{2,1,0:T(8,128)(2,1)} %get-tuple-element.12.u_hbm, bf16[4,2048,256]{2,1,0:T(8,128)(2,1)} %get-tuple-element.13.v_hbm, bf16[2048,256]{1,0:T(8,128)(2,1)} %get-tuple-element.14.r_hbm, bf16[4,2048,256]{2,1,0:T(8,128)(2,1)} %get-tuple-element.15.c_hbm, ...), custom_call_target="tpu_custom_call" | custom-call | flops 10000000000 | bytes 25165824 | tf_op jit(solution)/shard_map/recompress/pallas_call | solution.py:159
